TPU v7x, 512 devices: a whole 4x8x8 slice. The times are simulated.
512 devices in a mesh: seq: 16 (over y_lo, z), exp: 32 (over x, y_hi, core).
Axes of the slice: x: 4, y: 8 (y_hi: 4, y_lo: 2; y = y_hi * 2 + y_lo), z: 8, core: 2. Of those that a mesh axis runs over, the one named last changes fastest.
Arguments:
- resid: bfloat16 [32, 2048, 2048], P('exp', 'seq'), may hold values from -60 to 60
- norm_gain: float32 [2048], replicated, may hold values from 0.1 to 1.9
- router_logits: float32 [32, 2048, 32], P('exp', 'seq'), may hold values from -20 to 280
- router_weight: bfloat16 [2048, 32], replicated, may hold values from -0.125 to 0.125
- expert_index: int32 [32, 2048], P('exp', 'seq'), may hold values from 0 to 31, as said below
- slot: int32 [32, 2048], P('exp', 'seq'), may hold values from 0 to 3, as said below
- w_in: bfloat16 [32, 2048, 5120], P('exp', None, 'seq'), may hold values from -0.125 to 0.125
- w_out: bfloat16 [32, 5120, 2048], P('exp', 'seq'), may hold values from -0.078125 to 0.078125
- grad_out: bfloat16 [32, 2048, 2048], P('exp', 'seq'), may hold values from -6 to 6
- queries: bfloat16 [32, 2048, 2048], P('exp', 'seq'), may hold values from -6 to 6
- keys: bfloat16 [32, 64, 2048], P('exp', None, 'seq'), may hold values from -6 to 6
- values: bfloat16 [32, 64, 2048], P('exp', None, 'seq'), may hold values from -6 to 6
Outputs:
- grad_stream: bfloat16 [32, 2048, 2048], P('exp', 'seq')
- grad_keys: bfloat16 [32, 64, 2048], P('exp', None, 'seq')
- grad_values: bfloat16 [32, 64, 2048], P('exp', None, 'seq')
Inputs may be any that keep to these rules, and one draw needn't show every extreme that they name: `expert_index`: in every block of 128 tokens one expert, the same in all blocks, is named by more than 3 tokens. A token's slot is the number of earlier tokens of its block with the same expert_index, or 3 where that number is 3 or more.
All inputs are finite; a program needn't handle non-finite values.
Results may differ from a plain program's by a relative error of at most 0.018.
Values may be sent and summed in bfloat16 or wider, within the bound.
No kernel may reach another device: no remote copies, remote signals or barrier semaphores. Data moves between devices by JAX's collectives and lax.ppermute only.
A program may use at most 128 MiB of HBM per device.

v0:
```python
import jax
import jax.numpy as jnp
from jax import lax
from jax.sharding import PartitionSpec as P

HEADS = 32
HEAD_DIM = 64


EPSILON = 1e-06
SCORE_SCALE = 0.125
COEFF = 0.7978845608


def gelu_slope(hidden):
    tangent = jnp.tanh(COEFF * (hidden + 0.044715 * hidden * hidden * hidden))
    return 0.5 * (1.0 + tangent) + 0.5 * hidden * (1.0 - tangent * tangent) * COEFF * (
        1.0 + 0.134145 * hidden * hidden
    )


def gelu_value(hidden):
    tangent = jnp.tanh(COEFF * (hidden + 0.044715 * hidden * hidden * hidden))
    return 0.5 * hidden * (1.0 + tangent)


def body(
    resid,
    norm_gain,
    router_logits,
    router_weight,
    expert_index,
    slot,
    w_in,
    w_out,
    grad_out,
    queries,
    keys,
    values,
):
    n_exp = lax.axis_size("exp")
    n_seq = lax.axis_size("seq")
    tokens = resid.shape[1]
    model_width = resid.shape[2]
    local_experts = w_in.shape[0]
    experts = local_experts * n_exp
    capacity = max(2, 3 * tokens // (4 * experts))
    key_rows, value_rows = (
        lax.all_gather(keys[0], "seq", axis=1, tiled=True),
        lax.all_gather(values[0], "seq", axis=1, tiled=True),
    )
    stream = resid[0].astype(jnp.float32)
    root_mean = jnp.sqrt(jnp.mean(stream * stream, axis=-1, keepdims=True) + EPSILON)
    normed = stream / root_mean
    normed_in = (normed * norm_gain).astype(jnp.bfloat16)
    router_probs = jax.nn.softmax(router_logits[0], axis=-1)
    expert_ids = expert_index[0]
    slot_pos = slot[0]
    kept_mask = slot_pos < capacity
    onehot = (expert_ids[:, None] == jnp.arange(experts, dtype=jnp.int32)[None, :]).astype(
        jnp.float32
    )
    chosen = jnp.sum(router_probs * onehot, axis=-1)
    upstream = grad_out[0].astype(jnp.float32)
    target = jnp.where(kept_mask, expert_ids * capacity + slot_pos, -1)
    dispatch_table = (
        jnp.arange(experts * capacity, dtype=jnp.int32)[:, None] == target[None, :]
    ).astype(jnp.bfloat16)
    stacked = jnp.stack([normed_in, grad_out[0]], axis=0)
    outgoing = jnp.einsum(
        "st,ctd->scd", dispatch_table, stacked, preferred_element_type=jnp.float32
    ).astype(jnp.bfloat16)
    outgoing = outgoing.reshape(n_exp, local_experts, capacity, 2, model_width)
    arrived = lax.all_to_all(outgoing, "exp", split_axis=0, concat_axis=0, tiled=True)
    everything = lax.all_gather(arrived[None], "seq", axis=0, tiled=True)
    expert_block = everything[:, :, 0]
    slot_inputs = expert_block[:, :, :, 0, :].reshape(-1, model_width)
    slot_grads = expert_block[:, :, :, 1, :].reshape(-1, model_width)
    weight_in = w_in[0]
    hidden = jnp.dot(slot_inputs, weight_in, preferred_element_type=jnp.float32)
    hidden_grad = lax.dot_general(
        slot_grads, w_out[0], (((1,), (1,)), ((), ())), preferred_element_type=jnp.float32
    )
    scaled_grad = (hidden_grad * gelu_slope(hidden)).astype(jnp.bfloat16)
    gate_part = jnp.sum(gelu_value(hidden) * hidden_grad, axis=1).astype(jnp.bfloat16)
    partial_value = lax.dot_general(
        scaled_grad, weight_in, (((1,), (1,)), ((), ())), preferred_element_type=jnp.float32
    ).astype(jnp.bfloat16)
    per_expert = [partial_value.reshape(n_seq, n_exp, capacity, model_width)]
    per_gate = [gate_part.reshape(n_seq, n_exp, capacity)]
    partials = jnp.stack(per_expert, axis=2)
    gate_parts = jnp.stack(per_gate, axis=2)
    returned, returned_gate = (
        lax.all_to_all(
            lax.all_to_all(partials, "seq", split_axis=0, concat_axis=0, tiled=True),
            "exp",
            split_axis=1,
            concat_axis=1,
            tiled=True,
        ),
        lax.all_to_all(
            lax.all_to_all(gate_parts, "seq", split_axis=0, concat_axis=0, tiled=True),
            "exp",
            split_axis=1,
            concat_axis=1,
            tiled=True,
        ),
    )
    combined = jnp.sum(returned.astype(jnp.float32), axis=0).reshape(
        experts * capacity, model_width
    )
    gate_total = jnp.sum(returned_gate.astype(jnp.float32), axis=0).reshape(experts * capacity)
    safe_target = jnp.maximum(target, 0)
    dispatch_grad = jnp.where(kept_mask[:, None], chosen[:, None] * combined[safe_target], 0.0)
    prob_grad = jnp.where(kept_mask, gate_total[safe_target], 0.0)
    logit_grad = prob_grad[:, None] * chosen[:, None] * (onehot - router_probs)
    router_term = jnp.dot(
        logit_grad, router_weight.astype(jnp.float32).T, precision=lax.Precision.HIGHEST
    )
    normed_grad = (dispatch_grad + router_term) * norm_gain
    stream_grad = (
        upstream
        + (normed_grad - normed * jnp.mean(normed_grad * normed, axis=-1, keepdims=True))
        / root_mean
    )
    grad_stream = stream_grad.astype(jnp.bfloat16)
    query_heads = queries[0].reshape(tokens, HEADS, HEAD_DIM)
    key_heads = key_rows.reshape(-1, HEADS, HEAD_DIM)
    value_heads = value_rows.reshape(-1, HEADS, HEAD_DIM)
    context_heads = grad_stream.reshape(tokens, HEADS, HEAD_DIM)
    scores = (
        jnp.einsum("qhd,khd->hqk", query_heads, key_heads, preferred_element_type=jnp.float32)
        * SCORE_SCALE
    )
    att_probs = jax.nn.softmax(scores, axis=-1)
    prob_grads = jnp.einsum(
        "qhd,khd->hqk", context_heads, value_heads, preferred_element_type=jnp.float32
    )
    delta = jnp.sum(att_probs * prob_grads, axis=-1, keepdims=True)
    score_grads = att_probs * (prob_grads - delta)
    att_weights = att_probs.astype(jnp.bfloat16)
    score_weights = score_grads.astype(jnp.bfloat16)
    key_terms = (
        jnp.einsum("hqk,qhd->khd", score_weights, query_heads, preferred_element_type=jnp.float32)
        * SCORE_SCALE
    )
    value_terms = jnp.einsum(
        "hqk,qhd->khd", att_weights, context_heads, preferred_element_type=jnp.float32
    )
    encoder_total = key_terms.shape[0]
    owned_keys, owned_values = (
        lax.psum_scatter(
            key_terms.reshape(encoder_total, model_width).astype(jnp.bfloat16),
            "seq",
            scatter_dimension=1,
            tiled=True,
        ).astype(jnp.float32),
        lax.psum_scatter(
            value_terms.reshape(encoder_total, model_width).astype(jnp.bfloat16),
            "seq",
            scatter_dimension=1,
            tiled=True,
        ).astype(jnp.float32),
    )
    grad_keys = owned_keys.astype(jnp.bfloat16)
    grad_values = owned_values.astype(jnp.bfloat16)
    return (grad_stream[None], grad_keys[None], grad_values[None])


def solution(mesh):
    in_specs = (
        P("exp", "seq", None),
        P(),
        P("exp", "seq", None),
        P(),
        P("exp", "seq"),
        P("exp", "seq"),
        P("exp", None, "seq"),
        P("exp", "seq", None),
        P("exp", "seq", None),
        P("exp", "seq", None),
        P("exp", None, "seq"),
        P("exp", None, "seq"),
    )
    out_specs = (P("exp", "seq", None), P("exp", None, "seq"), P("exp", None, "seq"))
    return jax.shard_map(body, mesh=mesh, in_specs=in_specs, out_specs=out_specs, check_vma=False)
```

profile of v0, /device:TPU:6, one launch (start us, length us, event | category | flops | bytes accessed | tf_op | source)
XLA Modules:
  0.0 925.0 jit_solution(11984761067505608554)
XLA Ops:
  12.7 32.3 %all_to_all.25 = bf16[32,1,3,2,2048]{4,3,2,1,0:T(2,128)(2,1)} all-to-all(bf16[32,1,3,2,2048]{4,3,2,1,0:T(2,128)(2,1)S(1)} %bitcast.83), channel_id=1, replica_groups=mesh['seq'=16,'exp'=32] {'exp'}, dimensions={0} | all-to-all | bytes 1572864 | tf_op jit(solution)/shard_map/all_to_all | solution.py:74
  45.0 147.8 %all-gather.5.cloned.1.call-done = bf16[512,1,3,2,2048]{4,3,2,1,0:T(2,128)(2,1)} async-done(((bf16[32,1,3,2,2048]{4,3,2,1,0:T(2,128)(2,1)}), bf16[512,1,3,2,2048]{4,3,2,1,0:T(2,128)(2,1)}) %all-gather.5.cloned.1.call-update) | async-done | bytes 12582928 | tf_op jit(solution)/shard_map/all_gather | solution.py:75
  192.8 41.6 %slice_reduce_fusion = bf16[16,32,3,2048]{3,2,1,0:T(4,128)(2,1)} fusion(bf16[16,32,3,2,2048]{4,3,2,1,0:T(2,128)(2,1)} %bitcast.81), kind=kLoop, calls=%fused_computation.3 | loop fusion | bytes 12582912 | tf_op jit(solution)/shard_map/slice | solution.py:77
  234.4 46.2 %slice_reduce_fusion.1 = bf16[16,32,3,2048]{3,2,1,0:T(4,128)(2,1)} fusion(bf16[16,32,3,2,2048]{4,3,2,1,0:T(2,128)(2,1)} %bitcast.82), kind=kLoop, calls=%fused_computation.4 | loop fusion | bytes 12582912 | tf_op jit(solution)/shard_map/slice | solution.py:78
  280.6 16.3 %reshape_squeeze.10 = bf16[1536,2048]{1,0:T(8,128)(2,1)} reshape(bf16[16,32,3,2048]{3,2,1,0:T(4,128)(2,1)} %slice_reduce_fusion) | data formatting | bytes 12582912 | tf_op jit(solution)/shard_map/reshape;squeeze | solution.py:77
  296.9 16.3 %reshape_squeeze.9 = bf16[1536,2048]{1,0:T(8,128)(2,1)} reshape(bf16[16,32,3,2048]{3,2,1,0:T(4,128)(2,1)} %slice_reduce_fusion.1) | data formatting | bytes 12582912 | tf_op jit(solution)/shard_map/reshape;squeeze | solution.py:78
  313.2 5.2 fusion.14
  318.4 3.9 multiply_reduce_fusion
  323.4 4.4 all-to-all-start.3
  327.8 9.1 convolution_convert_fusion
  336.9 16.8 %stack_reshape.4 = bf16[16,32,1,3,2048]{4,3,1,0,2:T(4,128)(2,1)} reshape(bf16[1536,2048]{1,0:T(8,128)(2,1)} %convolution_convert_fusion) | data formatting | bytes 12582912 | tf_op jit(solution)/shard_map/stack;reshape | solution.py:91
  353.7 10.9 %copy.33 = bf16[16,32,1,3,2048]{4,1,3,2,0:T(8,128)(2,1)} copy(bf16[16,32,1,3,2048]{4,3,1,0,2:T(4,128)(2,1)} %stack_reshape.4) | data formatting | bytes 12582912 | tf_op jit(solution)/shard_map/stack;reshape | solution.py:91
  364.6 8.3 all-to-all-start.1
  373.6 155.7 %all-to-all-done.1 = bf16[16,32,1,3,2048]{4,1,3,2,0:T(8,128)(2,1)} async-done(((bf16[16,32,1,3,2048]{4,1,3,2,0:T(8,128)(2,1)}), bf16[16,32,1,3,2048]{4,1,3,2,0:T(8,128)(2,1)}, u32[]{:S(2)}, u32[]{:S(2)}) %all-to-all-start.1) | async-done | bytes 6291488 | tf_op jit(solution)/shard_map/all_to_all | solution.py:95
  529.3 9.3 %all-to-all-start.4 = ((bf16[16,32,1,3]{0,3,2,1:T(4,128)(2,1)}), bf16[16,32,1,3]{0,3,2,1:T(4,128)(2,1)S(1)}, u32[]{:S(2)}, u32[]{:S(2)}) async-start(bf16[16,32,1,3]{0,3,2,1:T(4,128)(2,1)} %copy.36), calls=%async_computation.4 | async-start | bytes 65536 | tf_op jit(solution)/shard_map/all_to_all | solution.py:101
  538.6 8.9 copy.34
  547.5 10.0 %all-to-all-start.2 = ((bf16[16,32,1,3,2048]{4,0,3,2,1:T(8,128)(2,1)}), bf16[16,32,1,3,2048]{4,0,3,2,1:T(8,128)(2,1)}, u32[]{:S(2)}, u32[]{:S(2)}) async-start(bf16[16,32,1,3,2048]{4,0,3,2,1:T(8,128)(2,1)} %copy.34), calls=%async_computation.2 | async-start | bytes 12582912 | tf_op jit(solution)/shard_map/all_to_all | solution.py:94
  557.6 164.3 %all-gather.1 = bf16[1,64,2048]{2,1,0:T(8,128)(2,1)S(1)} all-gather(bf16[1,64,128]{2,1,0:T(8,128)(2,1)S(1)} %copy-done.12), channel_id=3, replica_groups=mesh['seq'=16,'exp'=32] {'seq'}, dimensions={2}, use_global_device_ids=true | all-gather | bytes 278528 | tf_op jit(solution)/shard_map/all_gather | solution.py:49
  722.7 33.2 %all-gather.2 = bf16[1,64,2048]{2,1,0:T(8,128)(2,1)S(1)} all-gather(bf16[1,64,128]{2,1,0:T(8,128)(2,1)S(1)} %copy-done.13), channel_id=4, replica_groups=mesh['seq'=16,'exp'=32] {'seq'}, dimensions={2}, use_global_device_ids=true | all-gather | bytes 278528 | tf_op jit(solution)/shard_map/all_gather | solution.py:50
  759.8 5.9 convert_reduce_fusion
  769.7 2.8 multiply_reduce_fusion.1
  772.5 2.0 fusion.19
  777.2 66.7 %reduce-scatter.7.cloned.1.call-done = bf16[128,64]{1,0:T(8,128)(2,1)} async-done(((bf16[2048,64]{1,0:T(8,128)(2,1)}), bf16[128,64]{1,0:T(8,128)(2,1)}) %reduce-scatter.7.cloned.1.call-update) | async-done | bytes 16400
  845.4 71.2 %reduce-scatter.9.cloned.1.call-done = bf16[128,64]{1,0:T(8,128)(2,1)} async-done(((bf16[2048,64]{1,0:T(8,128)(2,1)}), bf16[128,64]{1,0:T(8,128)(2,1)}) %reduce-scatter.9.cloned.1.call-update) | async-done | bytes 16400
  (79 shorter events, 21.5 us)
Async XLA Ops:
  7.2 306.1 %copy-start = (bf16[1,2048,320]{1,2,0:T(8,128)(2,1)S(1)}, bf16[1,2048,320]{1,2,0:T(8,128)(2,1)}, u32[]{:S(2)}) copy-start(bf16[1,2048,320]{1,2,0:T(8,128)(2,1)} %param.18) | copy-start | bytes 3932164
  7.2 185.6 %all-gather.5.cloned.1.call-start = ((), (), s32[]{:S(2)}) async-start(), calls=%async_computation.7 | async-start | bytes 13369344 | tf_op jit(solution)/shard_map/all_gather | solution.py:75
  313.2 5.2 copy-start.2
  313.2 5.2 copy-start.17
  318.4 3.9 copy-start.18
  323.4 41.3 %all-to-all-start.3 = ((bf16[16,32,1,3]{1,3,2,0:T(4,128)(2,1)}), bf16[16,32,1,3]{1,3,2,0:T(4,128)(2,1)S(1)}, u32[]{:S(2)}, u32[]{:S(2)}) async-start(bf16[16,32,1,3]{1,3,2,0:T(4,128)(2,1)} %copy.35), calls=%async_computation.3 | async-start | bytes 32768 | tf_op jit(solution)/shard_map/all_to_all | solution.py:102
  364.6 164.7 %all-to-all-start.1 = ((bf16[16,32,1,3,2048]{4,1,3,2,0:T(8,128)(2,1)}), bf16[16,32,1,3,2048]{4,1,3,2,0:T(8,128)(2,1)}, u32[]{:S(2)}, u32[]{:S(2)}) async-start(bf16[16,32,1,3,2048]{4,1,3,2,0:T(8,128)(2,1)} %copy.33), calls=%async_computation.1 | async-start | bytes 12582912 | tf_op jit(solution)/shard_map/all_to_all | solution.py:95
  529.3 18.2 %all-to-all-start.4 = ((bf16[16,32,1,3]{0,3,2,1:T(4,128)(2,1)}), bf16[16,32,1,3]{0,3,2,1:T(4,128)(2,1)S(1)}, u32[]{:S(2)}, u32[]{:S(2)}) async-start(bf16[16,32,1,3]{0,3,2,1:T(4,128)(2,1)} %copy.36), calls=%async_computation.4 | async-start | bytes 65536 | tf_op jit(solution)/shard_map/all_to_all | solution.py:101
  547.5 10.1 %copy-start.12 = (bf16[1,64,128]{2,1,0:T(8,128)(2,1)S(1)}, bf16[1,64,128]{2,1,0:T(8,128)(2,1)}, u32[]{:S(2)}) copy-start(bf16[1,64,128]{2,1,0:T(8,128)(2,1)} %param.22) | copy-start | bytes 49156
  547.5 174.9 %copy-start.6 = (bf16[1,128,2048]{2,1,0:T(8,128)(2,1)S(1)}, bf16[1,128,2048]{2,1,0:T(8,128)(2,1)}, u32[]{:S(2)}) copy-start(bf16[1,128,2048]{2,1,0:T(8,128)(2,1)} %param.21) | copy-start | bytes 1572868
  547.5 212.3 %all-to-all-start.2 = ((bf16[16,32,1,3,2048]{4,0,3,2,1:T(8,128)(2,1)}), bf16[16,32,1,3,2048]{4,0,3,2,1:T(8,128)(2,1)}, u32[]{:S(2)}, u32[]{:S(2)}) async-start(bf16[16,32,1,3,2048]{4,0,3,2,1:T(8,128)(2,1)} %copy.34), calls=%async_computation.2 | async-start | bytes 12582912 | tf_op jit(solution)/shard_map/all_to_all | solution.py:94
  557.5 165.2 %copy-start.13 = (bf16[1,64,128]{2,1,0:T(8,128)(2,1)S(1)}, bf16[1,64,128]{2,1,0:T(8,128)(2,1)}, u32[]{:S(2)}) copy-start(bf16[1,64,128]{2,1,0:T(8,128)(2,1)} %param.23) | copy-start | bytes 49156
  557.5 198.9 %copy-start.11 = (f32[1,128,32]{1,2,0:T(8,128)S(1)}, f32[1,128,32]{1,2,0:T(8,128)}, u32[]{:S(2)}) copy-start(f32[1,128,32]{1,2,0:T(8,128)} %param.14) | copy-start | bytes 49156
  557.5 198.9 %copy-start.15 = (s32[1,128]{1,0:T(1,128)S(1)}, s32[1,128]{1,0:T(1,128)}, u32[]{:S(2)}) copy-start(s32[1,128]{1,0:T(1,128)} %param.16) | copy-start | bytes 1540
  557.5 199.0 %copy-start.16 = (s32[1,128]{1,0:T(1,128)S(1)}, s32[1,128]{1,0:T(1,128)}, u32[]{:S(2)}) copy-start(s32[1,128]{1,0:T(1,128)} %param.17) | copy-start | bytes 1540
  557.5 286.4 %reduce-scatter.7.cloned.1.call-start = ((), (), s32[]{:S(2)}) async-start(), calls=%async_computation.8 | async-start | bytes 557056
  722.6 37.1 %copy-start.7 = (bf16[1,128,2048]{1,2,0:T(8,128)(2,1)}, bf16[1,128,2048]{1,2,0:T(8,128)(2,1)S(1)}, u32[]{:S(2)}) copy-start(bf16[1,128,2048]{1,2,0:T(8,128)(2,1)S(1)} %copy.37) | copy-start | bytes 1572868
  767.1 1.9 copy-start.5
  769.4 3.1 copy-start.4
  769.7 2.8 copy-start.9
  769.7 2.8 copy-start.8
  772.5 3.1 copy-start.10
  775.5 142.5 %copy-start.1 = (bf16[1,2048,320]{1,2,0:T(8,128)(2,1)S(1)}, bf16[1,2048,320]{1,2,0:T(8,128)(2,1)}, u32[]{:S(2)}) copy-start(bf16[1,2048,320]{1,2,0:T(8,128)(2,1)} %param.18) | copy-start | bytes 3932164
  775.5 141.0 %reduce-scatter.9.cloned.1.call-start = ((), (), s32[]{:S(2)}) async-start(), calls=%async_computation.9 | async-start | bytes 557056
  (2 other events, 2.1 us)
Sparse Core Ops, SparseCore 0:
  45.2 147.6 all-gather.4
  775.7 68.2 reduce-scatter.6
  846.9 69.5 reduce-scatter.8
where the time goes:
time: 936 us; the launch traced here: 925 us
  waiting for transfers between devices  441 us (47%)
  blocking collectives  230 us (25%)
  local copies, waits for them, and re-layouts  168 us (18%)
  starting transfers between devices  32.1 us (3%)
  matrix products  29.3 us (3%)
  between operations  14.6 us (2%)
  other arithmetic  9.7 us (1%)
    all_gather x1, blocking collectives, body(): lax.all_gather(keys[0], 'seq', axis=1, tiled=True)  164 us
    all_to_all x1, waiting for transfers between devices, body(): lax.all_to_all(partials, 'seq', split_axis=0, concat_axis=0, tiled=True)  156 us
    all_gather x1, waiting for transfers between devices, body(): everything = lax.all_gather(arrived[None], 'seq', axis=0, tiled=True)  148 us
    unnamed x5, waiting for transfers between devices  138 us
    slice x1, local copies, waits for them, and re-layouts, body(): slot_grads = expert_block[:, :, :, 1, :].reshape(-1, model_width)  46.2 us
    slice x1, local copies, waits for them, and re-layouts, body(): slot_inputs = expert_block[:, :, :, 0, :].reshape(-1, model_width)  41.6 us
    all_gather x1, blocking collectives, body(): lax.all_gather(values[0], 'seq', axis=1, tiled=True)  33.2 us
    all_to_all x1, blocking collectives, body(): lax.all_to_all(outgoing, 'exp', split_axis=0, concat_axis=0, tiled=True)  32.3 us
  transfers between devices with their start and end apart: 7, of which 4 were waited for; matrix products, arithmetic and copies ran while one was open for 6% of the time, Pallas kernels for 0%

commit v1 on v0

v1 whole, which is shorter than its diff:
```python
import functools

import jax
import jax.numpy as jnp
from jax import lax
from jax.experimental import pallas as pl
from jax.experimental.pallas import tpu as pltpu
from jax.sharding import PartitionSpec as P

D = 2048
EXPERTS = 32
CAP = 3
SLOTS = EXPERTS * CAP
ENC = 64
TOK = 128
N_Y = 2
N_Z = 8
HID = 320
EPSILON = 1e-06
SCORE_SCALE = 0.125
COEFF = 0.7978845608
BF16 = jnp.bfloat16
F32 = jnp.float32
WIDE = D + 128
VMEM = 40 * 1024 * 1024


def dot(a, b, dims=((1,), (0,)), **kw):
    return lax.dot_general(a, b, (dims, ((), ())), preferred_element_type=F32, **kw)


def shuffle_matrix():
    row = lax.broadcasted_iota(jnp.int32, (512, 512), 0)
    col = lax.broadcasted_iota(jnp.int32, (512, 512), 1)
    return ((row // 16 == col % 32) & (row % 16 == col // 32)).astype(F32).astype(BF16)


def slot_table(ids, slot):
    target = jnp.where(slot < CAP, slot * EXPERTS + ids, -1)
    rows = lax.broadcasted_iota(jnp.int32, (SLOTS, TOK), 0)
    return (rows == target).astype(F32).astype(BF16)


def whole(shape):
    return pl.BlockSpec(shape, lambda i: (0,) * len(shape))


def call(kernel, ins, outs, in_specs=None, scratch=(), flops=0, name=None):
    in_specs = in_specs or [None] * len(ins)
    specs = [s or whole(a.shape) for s, a in zip(in_specs, ins)]
    moved = sum(a.size * a.dtype.itemsize for a in ins)
    moved += sum(o.size * o.dtype.itemsize for o in outs)
    return pl.pallas_call(
        kernel,
        grid=(1,),
        in_specs=specs,
        out_specs=[whole(o.shape) for o in outs],
        out_shape=outs,
        scratch_shapes=list(scratch),
        compiler_params=pltpu.CompilerParams(vmem_limit_bytes=VMEM),
        cost_estimate=pl.CostEstimate(flops=flops, bytes_accessed=moved, transcendentals=0),
        name=name,
    )(*ins)


def shape(dims, dtype=BF16):
    return jax.ShapeDtypeStruct(dims, dtype)


def dispatch_kernel(resid_ref, grad_ref, gain_ref, ids_ref, slot_ref, out_ref, rows_ref):
    stream = resid_ref[...].astype(F32)
    root_mean = jnp.sqrt(jnp.mean(stream * stream, axis=-1, keepdims=True) + EPSILON)
    normed_in = (stream / root_mean * gain_ref[...]).astype(BF16)
    table = slot_table(ids_ref[...], slot_ref[...])
    for half, source in enumerate((normed_in, grad_ref[...])):
        picked = dot(table, source).astype(BF16)
        for part in range(8):
            for c in range(CAP):
                row = (half * 8 + part) * 32
                rows_ref[row : row + 32, c * 256 : (c + 1) * 256] = picked[
                    c * 32 : (c + 1) * 32, part * 256 : (part + 1) * 256
                ]
    out_ref[...] = dot(shuffle_matrix(), rows_ref[...]).astype(BF16)


def collect_kernel(in_ref, kv_ref, kv_other_ref, out_ref):
    rows = dot(shuffle_matrix(), in_ref[...], ((0,), (0,))).astype(BF16)
    for half in range(2):
        for part in range(8):
            for c in range(CAP):
                row = (half * 8 + part) * 32
                out_ref[
                    half * 96 + c * 32 : half * 96 + (c + 1) * 32, part * 256 : (part + 1) * 256
                ] = rows[row : row + 32, c * 256 : (c + 1) * 256]
    for i in range(8):
        out_ref[192:208, i * 128 : (i + 1) * 128] = kv_ref[i * 16 : (i + 1) * 16, :]
        out_ref[192:208, (i + 8) * 128 : (i + 9) * 128] = kv_other_ref[i * 16 : (i + 1) * 16, :]


def expert_kernel(n, split, *refs):
    in_refs, grad_refs = refs[:n], refs[n : 2 * n]
    w_in_refs, w_out_refs = refs[2 * n : 2 * n + 2], refs[2 * n + 2 : 2 * n + 4]
    out_refs = refs[2 * n + 4 :]
    inputs = jnp.concatenate([r[...] for r in in_refs], axis=0) if n > 1 else in_refs[0][...]
    grads = jnp.concatenate([r[...] for r in grad_refs], axis=0) if n > 1 else grad_refs[0][...]
    total, gate = None, None
    for w_in_ref, w_out_ref in zip(w_in_refs, w_out_refs):
        hidden = dot(inputs, w_in_ref[...])
        hidden_grad = dot(grads, w_out_ref[...], ((1,), (1,)))
        square = hidden * hidden
        tangent = jnp.tanh(COEFF * (hidden + 0.044715 * square * hidden))
        half = 0.5 * (1.0 + tangent)
        slope = half + 0.5 * hidden * (1.0 - tangent * tangent) * COEFF * (1.0 + 0.134145 * square)
        scaled = (hidden_grad * slope).astype(BF16)
        part = dot(scaled, w_in_ref[...], ((1,), (1,)))
        gates = jnp.sum(half * hidden * hidden_grad, axis=1, keepdims=True)
        total = part if total is None else total + part
        gate = gates if gate is None else gate + gates
    total = total.astype(BF16)
    gate = jnp.broadcast_to(gate, (n * 96, 128)).astype(BF16)
    size = 48 if split else 96
    for i, out_ref in enumerate(out_refs):
        out_ref[:, :D] = total[i * size : (i + 1) * size]
        out_ref[:, D:] = gate[i * size : (i + 1) * size]


def experts(blocks, weights, split=False, name=None):
    n = len(blocks)
    ins = [b[0] for b in blocks] + [b[1] for b in blocks] + list(weights)
    specs = [pl.BlockSpec((96, D), lambda i, k=b[2]: (k, 0)) for b in blocks]
    specs += [pl.BlockSpec((96, D), lambda i, k=b[3]: (k, 0)) for b in blocks]
    specs += [None] * 4
    outs = [shape((48, WIDE))] * 2 if split else [shape((96, WIDE))] * n
    return call(
        functools.partial(expert_kernel, n, split),
        ins,
        outs,
        specs,
        flops=2 * n * 96 * D * 2 * HID * 3,
        name=name,
    )


def return_kernel(own_ref, up_ref, down_ref, out_ref, rows_ref):
    total = own_ref[...].astype(F32) + up_ref[...].astype(F32) + down_ref[...].astype(F32)
    total = total.astype(BF16)
    rows_ref[:, 384:] = jnp.zeros((512, 128), BF16)
    for c in range(CAP):
        for part in range(16):
            rows_ref[part * 32 : (part + 1) * 32, c * 128 : (c + 1) * 128] = total[
                c * 32 : (c + 1) * 32, part * 128 : (part + 1) * 128
            ]
        rows_ref[c * 32 : (c + 1) * 32, 384:] = total[c * 32 : (c + 1) * 32, D:]
    out_ref[...] = dot(shuffle_matrix(), rows_ref[...]).astype(BF16)


def stream_kernel(
    in_ref, resid_ref, grad_ref, gain_ref, logits_ref, weight_ref, ids_ref, slot_ref, out_ref,
    rows_ref,
):
    rows = dot(shuffle_matrix(), in_ref[...], ((0,), (0,))).astype(BF16)
    for c in range(CAP):
        for part in range(16):
            rows_ref[c * 32 : (c + 1) * 32, part * 128 : (part + 1) * 128] = rows[
                part * 32 : (part + 1) * 32, c * 128 : (c + 1) * 128
            ]
        rows_ref[c * 32 : (c + 1) * 32, D:] = rows[c * 32 : (c + 1) * 32, 384:]
    ids = ids_ref[...]
    fetched = dot(slot_table(ids, slot_ref[...]), rows_ref[...], ((0,), (0,)))
    prob_grad = fetched[:, D : D + 1]
    logits = logits_ref[...]
    powers = jnp.exp(logits - jnp.max(logits, axis=-1, keepdims=True))
    probs = powers / jnp.sum(powers, axis=-1, keepdims=True)
    by_expert = lax.broadcasted_iota(jnp.int32, (EXPERTS, TOK), 0) == ids
    eye = lax.broadcasted_iota(jnp.int32, (EXPERTS, EXPERTS), 0) == lax.broadcasted_iota(
        jnp.int32, (EXPERTS, EXPERTS), 1
    )
    onehot = dot(by_expert.astype(F32).astype(BF16), eye.astype(F32).astype(BF16), ((0,), (0,)))
    chosen = jnp.sum(probs * onehot, axis=-1, keepdims=True)
    logit_grad = prob_grad * chosen * (onehot - probs)
    router_term = dot(
        logit_grad, weight_ref[...].astype(F32), ((1,), (1,)), precision=lax.Precision.HIGHEST
    )
    stream = resid_ref[...].astype(F32)
    root_mean = jnp.sqrt(jnp.mean(stream * stream, axis=-1, keepdims=True) + EPSILON)
    normed = stream / root_mean
    normed_grad = (chosen * fetched[:, :D] + router_term) * gain_ref[...]
    mean = jnp.mean(normed_grad * normed, axis=-1, keepdims=True)
    out_ref[...] = (
        grad_ref[...].astype(F32) + (normed_grad - normed * mean) / root_mean
    ).astype(BF16)


def head_mask():
    row = lax.broadcasted_iota(jnp.int32, (256, 256), 0)
    col = lax.broadcasted_iota(jnp.int32, (256, 256), 1)
    return row // ENC == col // ENC


def by_head(rows, mask):
    return jnp.where(mask, jnp.concatenate([rows.astype(F32)] * 4, axis=0), 0.0).astype(BF16)


def probs_kernel(place_ref, *refs):
    block_refs, query_ref, probs_ref, values_ref, keys_ref = (
        refs[:8], refs[8], refs[9], refs[10], refs[11],
    )
    for i, block_ref in enumerate(block_refs):
        for other in range(2):
            lanes = pl.ds(pl.multiple_of(place_ref[2 * i + other] * 128, 128), 128)
            for k in range(4):
                base = (other * 8 + k) * 128
                keys_ref[k * 16 : (k + 1) * 16, lanes] = block_ref[:, base : base + 128]
                values_ref[k * 16 : (k + 1) * 16, lanes] = block_ref[:, base + 512 : base + 640]
    mask = head_mask()
    for g in range(8):
        cols = slice(g * 256, (g + 1) * 256)
        scores = dot(by_head(keys_ref[:, cols], mask), query_ref[:, cols], ((1,), (1,)))
        scores = (scores * SCORE_SCALE).reshape(4, ENC, TOK)
        powers = jnp.exp(scores - jnp.max(scores, axis=1, keepdims=True))
        probs = powers / jnp.sum(powers, axis=1, keepdims=True)
        probs_ref[g] = probs.reshape(256, TOK)


def attend_kernel(probs_ref, values_ref, query_ref, stream_ref, out_ref):
    mask = head_mask()
    for g in range(8):
        cols = slice(g * 256, (g + 1) * 256)
        probs = probs_ref[g]
        context, query = stream_ref[:, cols], query_ref[:, cols]
        prob_grads = dot(by_head(values_ref[:, cols], mask), context, ((1,), (1,)))
        delta = jnp.sum((probs * prob_grads).reshape(4, ENC, TOK), axis=1, keepdims=True)
        delta = jnp.broadcast_to(delta, (4, ENC, TOK)).reshape(256, TOK)
        score_weights = (probs * (prob_grads - delta)).astype(BF16)
        key_terms = jnp.where(mask, dot(score_weights, query), 0.0)
        value_terms = jnp.where(mask, dot(probs.astype(BF16), context), 0.0)
        key_terms = jnp.sum(key_terms.reshape(4, ENC, 256), axis=0) * SCORE_SCALE
        value_terms = jnp.sum(value_terms.reshape(4, ENC, 256), axis=0)
        for half in range(2):
            row = (2 * g + half) * 128
            lanes = slice(half * 128, (half + 1) * 128)
            out_ref[row : row + 64] = key_terms[:, lanes].astype(BF16)
            out_ref[row + 64 : row + 128] = value_terms[:, lanes].astype(BF16)


def seq_pairs(step):
    return [
        (y * N_Z + z, ((y + step[0]) % N_Y) * N_Z + (z + step[1]) % N_Z)
        for y in range(N_Y)
        for z in range(N_Z)
    ]


def shift(a, step):
    return lax.ppermute(a, "seq", seq_pairs(step))


UP, DOWN, ACROSS = (0, 1), (0, -1), (1, 0)


def plus(a, b):
    return (a.astype(F32) + b.astype(F32)).astype(BF16)


def body(
    resid,
    norm_gain,
    router_logits,
    router_weight,
    expert_index,
    slot,
    w_in,
    w_out,
    grad_out,
    queries,
    keys,
    values,
):
    seq = lax.axis_index("seq")
    gain = norm_gain.reshape(1, D)
    stream, upstream, query = resid[0], grad_out[0], queries[0]
    kv = jnp.concatenate([keys[0], values[0]], axis=0)
    kv_other = shift(kv, ACROSS)
    (outgoing,) = call(
        dispatch_kernel,
        [stream, upstream, gain, expert_index, slot],
        [shape((512, 768))],
        scratch=[pltpu.VMEM((512, 768), BF16)],
        flops=2 * 512 * 512 * 768,
        name="dispatch",
    )
    arrived = lax.all_to_all(outgoing, "exp", 0, 0, tiled=True)
    (block,) = call(
        collect_kernel,
        [arrived, kv, kv_other],
        [shape((208, D))],
        flops=2 * 512 * 512 * 768,
        name="collect",
    )
    block, own_in, own_out = lax.optimization_barrier((block, w_in[0], w_out[0]))
    ups, downs = [block], [block]
    for _ in range(3):
        ups.append(shift(ups[-1], UP))
        downs.append(shift(downs[-1], DOWN))
    far_in = shift(ups[3][:96], UP)
    far_grad = shift(downs[3][96:], DOWN)
    weights = (own_in, shift(own_in, ACROSS), own_out, shift(own_out, ACROSS))

    (own,) = experts([(block, block, 0, 1)], weights, name="experts_0")
    up_parts, down_parts = [own], [own]
    for k in (1, 2, 3):
        a, b = experts(
            [(ups[k], ups[k], 0, 1), (downs[k], downs[k], 0, 1)], weights, name=f"experts_{k}"
        )
        up_parts.append(a)
        down_parts.append(b)
    far_a, far_b = experts([(far_in, far_grad, 0, 0)], weights, split=True, name="experts_4")

    back, forth = shift(far_a, DOWN), shift(far_b, UP)
    back = jnp.concatenate([plus(up_parts[3][:48], back), up_parts[3][48:]], axis=0)
    forth = jnp.concatenate([down_parts[3][:48], plus(down_parts[3][48:], forth)], axis=0)
    for k in (2, 1):
        back = plus(shift(back, DOWN), up_parts[k])
        forth = plus(shift(forth, UP), down_parts[k])
    back, forth = shift(back, DOWN), shift(forth, UP)

    z, y = seq % N_Z, seq // N_Z
    places = []
    for step in (0, -1, 1, -2, 2, -3, 3, 4):
        at = (z + step + N_Z) % N_Z
        places += [y * N_Z + at, (1 - y) * N_Z + at]
    kv_blocks = [block, ups[1], downs[1], ups[2], downs[2], ups[3], downs[3], far_grad]
    probs, all_values = call(
        probs_kernel,
        [jnp.stack(places).astype(jnp.int32)] + kv_blocks + [query],
        [shape((8, 256, TOK), F32), shape((ENC, D))],
        [pl.BlockSpec(memory_space=pltpu.SMEM)]
        + [pl.BlockSpec((16, D), lambda i, k=k: (k, 0)) for k in [12] * 7 + [6]]
        + [None],
        scratch=[pltpu.VMEM((ENC, D), BF16)],
        flops=8 * 2 * 256 * 256 * 128,
        name="probs",
    )

    (returning,) = call(
        return_kernel,
        [own, back, forth],
        [shape((512, 512))],
        scratch=[pltpu.VMEM((512, 512), BF16)],
        flops=2 * 512 * 512 * 512,
        name="return",
    )
    returned = lax.all_to_all(returning, "exp", 0, 0, tiled=True)
    (grad_stream,) = call(
        stream_kernel,
        [
            returned, stream, upstream, gain, router_logits[0], router_weight, expert_index, slot,
        ],
        [shape((TOK, D))],
        scratch=[pltpu.VMEM((SLOTS, WIDE), BF16)],
        flops=2 * 512 * 512 * 512,
        name="stream",
    )
    (terms,) = call(
        attend_kernel,
        [probs, all_values, query, grad_stream],
        [shape((2048, 128))],
        flops=8 * 3 * 2 * 256 * 256 * 128,
        name="attend",
    )
    terms = lax.all_to_all(terms, "seq", 0, 0, tiled=True)
    totals = jnp.sum(terms.reshape(16, 2, ENC, 128).astype(F32), axis=0).astype(BF16)
    return (grad_stream[None], totals[0][None], totals[1][None])


def solution(mesh):
    in_specs = (
        P("exp", "seq", None),
        P(),
        P("exp", "seq", None),
        P(),
        P("exp", "seq"),
        P("exp", "seq"),
        P("exp", None, "seq"),
        P("exp", "seq", None),
        P("exp", "seq", None),
        P("exp", "seq", None),
        P("exp", None, "seq"),
        P("exp", None, "seq"),
    )
    out_specs = (P("exp", "seq", None), P("exp", None, "seq"), P("exp", None, "seq"))
    return jax.shard_map(body, mesh=mesh, in_specs=in_specs, out_specs=out_specs, check_vma=False)
```

time: 936 us -> 266 us (0.28)
  waiting for transfers between devices: 441 us -> 86.1 us
  blocking collectives: 230 us -> 22.4 us
  local copies, waits for them, and re-layouts: 168 us -> 25.9 us
  starting transfers between devices: 32.1 us -> 91.4 us
  Pallas kernels: 0 us -> 34.9 us
  matrix products: 29.3 us -> 0 us
  between operations: 14.6 us -> 1.34 us
    all_gather x2 -> x0, blocking collectives: 197 us -> none  [the longest x1 164 us: body(): lax.all_gather(keys[0], 'seq', axis=1, tiled=True)]
    all_gather x1 -> x0, waiting for transfers between devices: 148 us -> none  [body(): everything = lax.all_gather(arrived[None], 'seq', axis=0, tiled=True)]
    all_to_all x4 -> x2, waiting for transfers between devices: 156 us -> 13.8 us  [the longest x1 9.18 us: body(): returned = lax.all_to_all(returning, 'exp', 0, 0, tiled=True)]
    unnamed x5 -> x0, waiting for transfers between devices: 138 us -> none
    slice x2 -> x5, local copies, waits for them, and re-layouts: 87.8 us -> 2.28 us  [the longest x1 0.85 us: body(): far_grad = shift(downs[3][96:], DOWN)]
    ppermute x0 -> x19, starting transfers between devices: none -> 73.9 us  [shift(): return lax.ppermute(a, 'seq', seq_pairs(step))]
    ppermute x0 -> x19, waiting for transfers between devices: none -> 72.3 us  [shift(): return lax.ppermute(a, 'seq', seq_pairs(step))]
    another operation x4 -> x1, local copies, waits for them, and re-layouts: 60.3 us -> 0.1 us  [body(): jnp.stack(places).astype(jnp.int32)]
  transfers between devices with their start and end apart: 7 -> 21, of which waited for: 4 -> 13; matrix products, arithmetic and copies ran while one was open for 6% -> 3% of each run, Pallas kernels for 0% -> 8%
where the time goes in v1:
time: 266 us; the launch traced here: 263 us
  starting transfers between devices  91.4 us (34%)
  waiting for transfers between devices  86.1 us (32%)
  Pallas kernels  34.9 us (13%)
  local copies, waits for them, and re-layouts  25.9 us (10%)
  blocking collectives  22.4 us (8%)
    ppermute x19, starting transfers between devices, shift(): return lax.ppermute(a, 'seq', seq_pairs(step))  73.9 us
    ppermute x19, waiting for transfers between devices, shift(): return lax.ppermute(a, 'seq', seq_pairs(step))  72.3 us
    pallas_call x11, Pallas kernels, call(): pl.pallas_call(kernel, grid=(1,), in_specs=specs, out_specs=[whole(o.shap...  34.9 us
    all_to_all x1, blocking collectives, body(): terms = lax.all_to_all(terms, 'seq', 0, 0, tiled=True)  22.4 us
    unnamed x79, local copies, waits for them, and re-layouts  20.1 us
    all_to_all x1, starting transfers between devices, body(): arrived = lax.all_to_all(outgoing, 'exp', 0, 0, tiled=True)  10.2 us
    all_to_all x1, waiting for transfers between devices, body(): returned = lax.all_to_all(returning, 'exp', 0, 0, tiled=True)  9.18 us
    all_to_all x1, starting transfers between devices, body(): returned = lax.all_to_all(returning, 'exp', 0, 0, tiled=True)  7.31 us
  transfers between devices with their start and end apart: 21, of which 13 were waited for; matrix products, arithmetic and copies ran while one was open for 3% of the time, Pallas kernels for 8%

profile of v1, /device:TPU:6, one launch (start us, length us, event | category | flops | bytes accessed | tf_op | source)
XLA Modules:
  0.0 262.8 jit_solution(2714262651613795623)
XLA Ops:
  6.7 10.2 %all-to-all-start = ((bf16[32,16,768]{2,1,0:T(8,128)(2,1)}), bf16[32,16,768]{2,1,0:T(8,128)(2,1)S(1)}, u32[]{:S(2)}, u32[]{:S(2)}) async-start(bf16[32,16,768]{2,1,0:T(8,128)(2,1)} %bitcast.3), calls=%async_computation | async-start | bytes 1572864 | tf_op jit(solution)/shard_map/all_to_all | solution.py:292
  21.4 13.1 %collective-permute-done.kv_other_ref = bf16[128,128]{1,0:T(8,128)(2,1)S(1)} collective-permute-done((bf16[128,128]{1,0:T(8,128)(2,1)S(1)}, bf16[128,128]{1,0:T(8,128)(2,1)S(1)}, u32[]{:S(2)}, u32[]{:S(2)}) %collective-permute-start) | collective-permute-done | bytes 32800 | tf_op jit(solution)/shard_map/ppermute | solution.py:255
  34.5 4.7 %all-to-all-done = bf16[32,16,768]{2,1,0:T(8,128)(2,1)S(1)} async-done(((bf16[32,16,768]{2,1,0:T(8,128)(2,1)}), bf16[32,16,768]{2,1,0:T(8,128)(2,1)S(1)}, u32[]{:S(2)}, u32[]{:S(2)}) %all-to-all-start) | async-done | bytes 786464 | tf_op jit(solution)/shard_map/all_to_all | solution.py:292
  39.8 10.9 %collective-permute-start.6 = (bf16[208,2048]{1,0:T(8,128)(2,1)S(1)}, bf16[208,2048]{1,0:T(8,128)(2,1)S(1)}, u32[]{:S(2)}, u32[]{:S(2)}) collective-permute-start(bf16[208,2048]{1,0:T(8,128)(2,1)S(1)} %collect.1.refs_0_.refs_1_), channel_id=1, source_target_pairs={{0,224},{32,0},{64,32},{96,64},{128,96},{160,128},{192,160},{224,1... | collective-permute-start | bytes 2555912 | tf_op jit(solution)/shard_map/ppermute | solution.py:255
  53.6 15.4 %collective-permute-done.6.refs_1_.refs_3_.refs_2_ = bf16[208,2048]{1,0:T(8,128)(2,1)S(1)} collective-permute-done((bf16[208,2048]{1,0:T(8,128)(2,1)S(1)}, bf16[208,2048]{1,0:T(8,128)(2,1)S(1)}, u32[]{:S(2)}, u32[]{:S(2)}) %collective-permute-start.6) | collective-permute-done | bytes 852000 | tf_op jit(solution)/shard_map/ppermute | solution.py:255
  69.1 5.6 %collective-permute-start.7 = (bf16[208,2048]{1,0:T(8,128)(2,1)S(1)}, bf16[208,2048]{1,0:T(8,128)(2,1)}, u32[]{:S(2)}, u32[]{:S(2)}) collective-permute-start(bf16[208,2048]{1,0:T(8,128)(2,1)S(1)} %collective-permute-done.6.refs_1_.refs_3_.refs_2_), channel_id=1, source_target_pairs={{0,224},{32,0},{64,32},{96,64},{128,96},{160,128},{192,160},{224,1... | collective-permute-start | bytes 2555912 | tf_op jit(solution)/shard_map/ppermute | solution.py:255
  84.0 8.0 %collective-permute-done.7.refs_1_.refs_3_.refs_4_ = bf16[208,2048]{1,0:T(8,128)(2,1)} collective-permute-done((bf16[208,2048]{1,0:T(8,128)(2,1)S(1)}, bf16[208,2048]{1,0:T(8,128)(2,1)}, u32[]{:S(2)}, u32[]{:S(2)}) %collective-permute-start.7) | collective-permute-done | bytes 852000 | tf_op jit(solution)/shard_map/ppermute | solution.py:255
  92.1 5.7 %collective-permute-start.8 = (bf16[208,2048]{1,0:T(8,128)(2,1)}, bf16[208,2048]{1,0:T(8,128)(2,1)S(1)}, u32[]{:S(2)}, u32[]{:S(2)}) collective-permute-start(bf16[208,2048]{1,0:T(8,128)(2,1)} %collective-permute-done.7.refs_1_.refs_3_.refs_4_), channel_id=1, source_target_pairs={{0,224},{32,0},{64,32},{96,64},{128,96},{160,128},{192,160},{224,1... | collective-permute-start | bytes 2555912 | tf_op jit(solution)/shard_map/ppermute | solution.py:255
  99.7 14.9 %collective-permute-done.8.refs_1_.refs_3_.refs_6_ = bf16[208,2048]{1,0:T(8,128)(2,1)S(1)} collective-permute-done((bf16[208,2048]{1,0:T(8,128)(2,1)}, bf16[208,2048]{1,0:T(8,128)(2,1)S(1)}, u32[]{:S(2)}, u32[]{:S(2)}) %collective-permute-start.8) | collective-permute-done | bytes 852000 | tf_op jit(solution)/shard_map/ppermute | solution.py:255
  115.4 5.5 %collective-permute-start.10 = (bf16[112,2048]{1,0:T(8,128)(2,1)}, bf16[112,2048]{1,0:T(8,128)(2,1)}, u32[]{:S(2)}, u32[]{:S(2)}) collective-permute-start(bf16[112,2048]{1,0:T(8,128)(2,1)} %slice.41), channel_id=1, source_target_pairs={{0,224},{32,0},{64,32},{96,64},{128,96},{160,128},{192,160},{224,1... | collective-permute-start | bytes 1376264 | tf_op jit(solution)/shard_map/ppermute | solution.py:255
  126.4 11.5 %collective-permute-done.2.refs_5_.refs_7_ = bf16[320,2048]{1,0:T(8,128)(2,1)} collective-permute-done((bf16[320,2048]{1,0:T(8,128)(2,1)}, bf16[320,2048]{1,0:T(8,128)(2,1)}, u32[]{:S(2)}, u32[]{:S(2)}) %collective-permute-start.2) | collective-permute-done | bytes 1310752 | tf_op jit(solution)/shard_map/ppermute | solution.py:255
  140.3 4.8 %experts_1.1 = (bf16[96,2176]{1,0:T(8,128)(2,1)S(1)}, bf16[96,2176]{1,0:T(8,128)(2,1)S(1)}) custom-call(bf16[208,2048]{1,0:T(8,128)(2,1)S(1)} %copy-done.13, bf16[208,2048]{1,0:T(8,128)(2,1)S(1)} %copy-done.10, bf16[208,2048]{1,0:T(8,128)(2,1)S(1)} %copy-done.13, bf16[208,2048]{1,0:T(8,128)(2,1)S(1)} %copy-done.10, bf16[2048,320]{1,0:T(8,128)(2,1)S(1)} %bitcast.36, ...), custom_call_target="tpu_custom_call" | custom-call | flops 1509949440 | bytes 9486336 | tf_op jit(solution)/shard_map/experts_1/pallas_call | solution.py:53
  145.1 4.7 %experts_4.1 = (bf16[48,2176]{1,0:T(8,128)(2,1)S(1)}, bf16[48,2176]{1,0:T(8,128)(2,1)S(1)}) custom-call(bf16[96,2048]{1,0:T(8,128)(2,1)} %collective-permute-done.9.refs_0_, bf16[112,2048]{1,0:T(8,128)(2,1)} %collective-permute-done.10.refs_1_.refs_7_, bf16[2048,320]{1,0:T(8,128)(2,1)S(1)} %bitcast.37, bf16[2048,320]{1,0:T(8,128)(2,1)S(1)} %copy.20.refs_3_.refs_5_, ...), custom_call_target="tpu_custom_call" | custom-call | flops 754974720 | bytes 6512640 | tf_op jit(solution)/shard_map/experts_4/pallas_call | solution.py:53
  152.1 5.3 %experts_2.1 = (bf16[96,2176]{1,0:T(8,128)(2,1)S(1)}, bf16[96,2176]{1,0:T(8,128)(2,1)S(1)}) custom-call(bf16[208,2048]{1,0:T(8,128)(2,1)} %collective-permute-done.4.refs_0_.refs_2_.refs_3_, bf16[208,2048]{1,0:T(8,128)(2,1)} %collective-permute-done.7.refs_1_.refs_3_.refs_4_, bf16[208,2048]{1,0:T(8,128)(2,1)} %collective-permute-done.4.refs_0_.refs_2_.refs_3_, ...), custom_call_target="tpu_custom_call" | custom-call | flops 1509949440 | bytes 9486336 | tf_op jit(solution)/shard_map/experts_2/pallas_call | solution.py:53
  157.4 4.9 %experts_3.1 = (bf16[96,2176]{1,0:T(8,128)(2,1)S(1)}, bf16[96,2176]{1,0:T(8,128)(2,1)S(1)}) custom-call(bf16[208,2048]{1,0:T(8,128)(2,1)S(1)} %copy-done.7, bf16[208,2048]{1,0:T(8,128)(2,1)S(1)} %copy-done.4, bf16[208,2048]{1,0:T(8,128)(2,1)S(1)} %copy-done.7, bf16[208,2048]{1,0:T(8,128)(2,1)S(1)} %copy-done.4, bf16[2048,320]{1,0:T(8,128)(2,1)S(1)} %bitcast.39, ...), custom_call_target="tpu_custom_call" | custom-call | flops 1509949440 | bytes 9486336 | tf_op jit(solution)/shard_map/experts_3/pallas_call | solution.py:53
  162.4 5.1 %collective-permute-start.11 = (bf16[48,2176]{1,0:T(8,128)(2,1)S(1)}, bf16[48,2176]{1,0:T(8,128)(2,1)S(1)}, u32[]{:S(2)}, u32[]{:S(2)}) collective-permute-start(bf16[48,2176]{1,0:T(8,128)(2,1)S(1)} %get-tuple-element.20), channel_id=1, source_target_pairs={{0,224},{32,0},{64,32},{96,64},{128,96},{160,128},{192,160},{224,1... | collective-permute-start | bytes 626696 | tf_op jit(solution)/shard_map/ppermute | solution.py:255
  170.9 5.6 %collective-permute-start.12 = (bf16[96,2176]{1,0:T(8,128)(2,1)S(1)}, bf16[96,2176]{1,0:T(8,128)(2,1)S(1)}, u32[]{:S(2)}, u32[]{:S(2)}) collective-permute-start(bf16[96,2176]{1,0:T(8,128)(2,1)S(1)} %pad_maximum_fusion), channel_id=1, source_target_pairs={{0,224},{32,0},{64,32},{96,64},{128,96},{160,128},{192,160},{224,1... | collective-permute-start | bytes 1253384 | tf_op jit(solution)/shard_map/ppermute | solution.py:255
  182.2 5.7 %collective-permute-start.13 = (bf16[96,2176]{1,0:T(8,128)(2,1)S(1)}, bf16[96,2176]{1,0:T(8,128)(2,1)S(1)}, u32[]{:S(2)}, u32[]{:S(2)}) collective-permute-start(bf16[96,2176]{1,0:T(8,128)(2,1)S(1)} %add_convert_fusion.3), channel_id=1, source_target_pairs={{0,224},{32,0},{64,32},{96,64},{128,96},{160,128},{192,160},{224,1... | collective-permute-start | bytes 1253384 | tf_op jit(solution)/shard_map/ppermute | solution.py:255
  193.6 5.6 %collective-permute-start.14 = (bf16[96,2176]{1,0:T(8,128)(2,1)S(1)}, bf16[96,2176]{1,0:T(8,128)(2,1)S(1)}, u32[]{:S(2)}, u32[]{:S(2)}) collective-permute-start(bf16[96,2176]{1,0:T(8,128)(2,1)S(1)} %add_convert_fusion.2), channel_id=1, source_target_pairs={{0,224},{32,0},{64,32},{96,64},{128,96},{160,128},{192,160},{224,1... | collective-permute-start | bytes 1253384 | tf_op jit(solution)/shard_map/ppermute | solution.py:255
  199.2 4.4 %experts_0.1.own_ref = bf16[96,2176]{1,0:T(8,128)(2,1)S(1)} custom-call(bf16[208,2048]{1,0:T(8,128)(2,1)S(1)} %copy-done.1, bf16[208,2048]{1,0:T(8,128)(2,1)S(1)} %copy-done.1, bf16[2048,320]{1,0:T(8,128)(2,1)S(1)} %bitcast.40, bf16[2048,320]{1,0:T(8,128)(2,1)S(1)} %copy.20.refs_3_.refs_5_, bf16[320,2048]{1,0:T(8,128)(2,1)} %bitcast.8.refs_4_.refs_6_, ...), custom_call_target="tpu_custom_call" | custom-call | flops 754974720 | bytes 7364608 | tf_op jit(solution)/shard_map/experts_0/pallas_call | solution.py:53
  206.1 7.3 %all-to-all-start.1 = ((bf16[32,16,512]{2,1,0:T(8,128)(2,1)}), bf16[32,16,512]{2,1,0:T(8,128)(2,1)}, u32[]{:S(2)}, u32[]{:S(2)}) async-start(bf16[32,16,512]{2,1,0:T(8,128)(2,1)} %bitcast.46), calls=%async_computation.1 | async-start | bytes 1048576 | tf_op jit(solution)/shard_map/all_to_all | solution.py:353
  220.4 9.2 %all-to-all-done.1 = bf16[32,16,512]{2,1,0:T(8,128)(2,1)} async-done(((bf16[32,16,512]{2,1,0:T(8,128)(2,1)}), bf16[32,16,512]{2,1,0:T(8,128)(2,1)}, u32[]{:S(2)}, u32[]{:S(2)}) %all-to-all-start.1) | async-done | bytes 524320 | tf_op jit(solution)/shard_map/all_to_all | solution.py:353
  232.7 4.2 %stream.1.stream_ref = bf16[128,2048]{1,0:T(8,128)(2,1)} custom-call(bf16[512,512]{1,0:T(8,128)(2,1)} %bitcast.10.in_ref, bf16[128,2048]{1,0:T(8,128)(2,1)S(1)} %bitcast.43, bf16[128,2048]{1,0:T(8,128)(2,1)S(1)} %bitcast.45, f32[1,2048]{1,0:T(1,128)S(1)} %bitcast.53, f32[128,32]{1,0:T(8,128)S(1)} %bitcast.51, bf16[2048,32]{1,0:T(8,128)(2,1)S(1)} %copy-done.19, ...), custom_call_target="tpu_custom_call" | custom-call | flops 268435456 | bytes 2253824 | tf_op jit(solution)/shard_map/stream/pallas_call | solution.py:53
  239.7 22.4 %all_to_all.31 = bf16[16,128,128]{2,1,0:T(8,128)(2,1)S(1)} all-to-all(bf16[16,128,128]{2,1,0:T(8,128)(2,1)S(1)} %bitcast.48), channel_id=1, replica_groups=mesh['seq'=16,'exp'=32] {'seq'}, dimensions={0} | all-to-all | bytes 1048576 | tf_op jit(solution)/shard_map/all_to_all | solution.py:371
  (127 shorter events, 66.6 us)
Async XLA Ops:
  6.7 32.5 %all-to-all-start = ((bf16[32,16,768]{2,1,0:T(8,128)(2,1)}), bf16[32,16,768]{2,1,0:T(8,128)(2,1)S(1)}, u32[]{:S(2)}, u32[]{:S(2)}) async-start(bf16[32,16,768]{2,1,0:T(8,128)(2,1)} %bitcast.3), calls=%async_computation | async-start | bytes 1572864 | tf_op jit(solution)/shard_map/all_to_all | solution.py:292
  17.0 17.5 %collective-permute-start = (bf16[128,128]{1,0:T(8,128)(2,1)S(1)}, bf16[128,128]{1,0:T(8,128)(2,1)S(1)}, u32[]{:S(2)}, u32[]{:S(2)}) collective-permute-start(bf16[128,128]{1,0:T(8,128)(2,1)S(1)} %pad_maximum_fusion.2.kv_ref), channel_id=1, source_target_pairs={{0,256},{32,288},{64,320},{96,352},{128,384},{160,416},{192,448},{... | collective-permute-start | bytes 98312 | tf_op jit(solution)/shard_map/ppermute | solution.py:255
  39.8 29.2 %collective-permute-start.6 = (bf16[208,2048]{1,0:T(8,128)(2,1)S(1)}, bf16[208,2048]{1,0:T(8,128)(2,1)S(1)}, u32[]{:S(2)}, u32[]{:S(2)}) collective-permute-start(bf16[208,2048]{1,0:T(8,128)(2,1)S(1)} %collect.1.refs_0_.refs_1_), channel_id=1, source_target_pairs={{0,224},{32,0},{64,32},{96,64},{128,96},{160,128},{192,160},{224,1... | collective-permute-start | bytes 2555912 | tf_op jit(solution)/shard_map/ppermute | solution.py:255
  50.8 23.9 %collective-permute-start.3 = (bf16[208,2048]{1,0:T(8,128)(2,1)S(1)}, bf16[208,2048]{1,0:T(8,128)(2,1)S(1)}, u32[]{:S(2)}, u32[]{:S(2)}) collective-permute-start(bf16[208,2048]{1,0:T(8,128)(2,1)S(1)} %collect.1.refs_0_.refs_1_), channel_id=1, source_target_pairs={{0,32},{32,64},{64,96},{96,128},{128,160},{160,192},{192,224},{224... | collective-permute-start | bytes 2555912 | tf_op jit(solution)/shard_map/ppermute | solution.py:255
  69.1 23.0 %collective-permute-start.7 = (bf16[208,2048]{1,0:T(8,128)(2,1)S(1)}, bf16[208,2048]{1,0:T(8,128)(2,1)}, u32[]{:S(2)}, u32[]{:S(2)}) collective-permute-start(bf16[208,2048]{1,0:T(8,128)(2,1)S(1)} %collective-permute-done.6.refs_1_.refs_3_.refs_2_), channel_id=1, source_target_pairs={{0,224},{32,0},{64,32},{96,64},{128,96},{160,128},{192,160},{224,1... | collective-permute-start | bytes 2555912 | tf_op jit(solution)/shard_map/ppermute | solution.py:255
  74.7 23.1 %collective-permute-start.4 = (bf16[208,2048]{1,0:T(8,128)(2,1)S(1)}, bf16[208,2048]{1,0:T(8,128)(2,1)}, u32[]{:S(2)}, u32[]{:S(2)}) collective-permute-start(bf16[208,2048]{1,0:T(8,128)(2,1)S(1)} %collective-permute-done.3.refs_0_.refs_2_.refs_1_), channel_id=1, source_target_pairs={{0,32},{32,64},{64,96},{96,128},{128,160},{160,192},{192,224},{224... | collective-permute-start | bytes 2555912 | tf_op jit(solution)/shard_map/ppermute | solution.py:255
  78.2 46.4 %collective-permute-start.1 = (bf16[2048,320]{0,1:T(8,128)(2,1)}, bf16[2048,320]{0,1:T(8,128)(2,1)}, u32[]{:S(2)}, u32[]{:S(2)}) collective-permute-start(bf16[2048,320]{0,1:T(8,128)(2,1)} %copy.19), channel_id=1, source_target_pairs={{0,256},{32,288},{64,320},{96,352},{128,384},{160,416},{192,448},{... | collective-permute-start | bytes 3932168 | tf_op jit(solution)/shard_map/ppermute | solution.py:255
  80.1 57.8 %collective-permute-start.2 = (bf16[320,2048]{1,0:T(8,128)(2,1)}, bf16[320,2048]{1,0:T(8,128)(2,1)}, u32[]{:S(2)}, u32[]{:S(2)}) collective-permute-start(bf16[320,2048]{1,0:T(8,128)(2,1)} %bitcast.8.refs_4_.refs_6_), channel_id=1, source_target_pairs={{0,256},{32,288},{64,320},{96,352},{128,384},{160,416},{192,448},{... | collective-permute-start | bytes 3932168 | tf_op jit(solution)/shard_map/ppermute | solution.py:255
  92.1 22.5 %collective-permute-start.8 = (bf16[208,2048]{1,0:T(8,128)(2,1)}, bf16[208,2048]{1,0:T(8,128)(2,1)S(1)}, u32[]{:S(2)}, u32[]{:S(2)}) collective-permute-start(bf16[208,2048]{1,0:T(8,128)(2,1)} %collective-permute-done.7.refs_1_.refs_3_.refs_4_), channel_id=1, source_target_pairs={{0,224},{32,0},{64,32},{96,64},{128,96},{160,128},{192,160},{224,1... | collective-permute-start | bytes 2555912 | tf_op jit(solution)/shard_map/ppermute | solution.py:255
  97.8 23.1 %collective-permute-start.5 = (bf16[208,2048]{1,0:T(8,128)(2,1)}, bf16[208,2048]{1,0:T(8,128)(2,1)S(1)}, u32[]{:S(2)}, u32[]{:S(2)}) collective-permute-start(bf16[208,2048]{1,0:T(8,128)(2,1)} %collective-permute-done.4.refs_0_.refs_2_.refs_3_), channel_id=1, source_target_pairs={{0,32},{32,64},{64,96},{96,128},{128,160},{160,192},{192,224},{224... | collective-permute-start | bytes 2555912 | tf_op jit(solution)/shard_map/ppermute | solution.py:255
  115.4 29.7 %collective-permute-start.10 = (bf16[112,2048]{1,0:T(8,128)(2,1)}, bf16[112,2048]{1,0:T(8,128)(2,1)}, u32[]{:S(2)}, u32[]{:S(2)}) collective-permute-start(bf16[112,2048]{1,0:T(8,128)(2,1)} %slice.41), channel_id=1, source_target_pairs={{0,224},{32,0},{64,32},{96,64},{128,96},{160,128},{192,160},{224,1... | collective-permute-start | bytes 1376264 | tf_op jit(solution)/shard_map/ppermute | solution.py:255
  122.6 22.5 %collective-permute-start.9 = (bf16[96,2048]{1,0:T(8,128)(2,1)}, bf16[96,2048]{1,0:T(8,128)(2,1)}, u32[]{:S(2)}, u32[]{:S(2)}) collective-permute-start(bf16[96,2048]{1,0:T(8,128)(2,1)} %slice.40), channel_id=1, source_target_pairs={{0,32},{32,64},{64,96},{96,128},{128,160},{160,192},{192,224},{224... | collective-permute-start | bytes 1179656 | tf_op jit(solution)/shard_map/ppermute | solution.py:255
  149.8 17.7 %collective-permute-start.15 = (bf16[48,2176]{1,0:T(8,128)(2,1)S(1)}, bf16[48,2176]{1,0:T(8,128)(2,1)S(1)}, u32[]{:S(2)}, u32[]{:S(2)}) collective-permute-start(bf16[48,2176]{1,0:T(8,128)(2,1)S(1)} %get-tuple-element.24), channel_id=1, source_target_pairs={{0,32},{32,64},{64,96},{96,128},{128,160},{160,192},{192,224},{224... | collective-permute-start | bytes 626696 | tf_op jit(solution)/shard_map/ppermute | solution.py:255
  162.4 8.4 %collective-permute-start.11 = (bf16[48,2176]{1,0:T(8,128)(2,1)S(1)}, bf16[48,2176]{1,0:T(8,128)(2,1)S(1)}, u32[]{:S(2)}, u32[]{:S(2)}) collective-permute-start(bf16[48,2176]{1,0:T(8,128)(2,1)S(1)} %get-tuple-element.20), channel_id=1, source_target_pairs={{0,224},{32,0},{64,32},{96,64},{128,96},{160,128},{192,160},{224,1... | collective-permute-start | bytes 626696 | tf_op jit(solution)/shard_map/ppermute | solution.py:255
  167.7 11.9 %collective-permute-start.16 = (bf16[96,2176]{1,0:T(8,128)(2,1)S(1)}, bf16[96,2176]{1,0:T(8,128)(2,1)S(1)}, u32[]{:S(2)}, u32[]{:S(2)}) collective-permute-start(bf16[96,2176]{1,0:T(8,128)(2,1)S(1)} %pad_maximum_fusion.1), channel_id=1, source_target_pairs={{0,32},{32,64},{64,96},{96,128},{128,160},{160,192},{192,224},{224... | collective-permute-start | bytes 1253384 | tf_op jit(solution)/shard_map/ppermute | solution.py:255
  170.9 11.1 %collective-permute-start.12 = (bf16[96,2176]{1,0:T(8,128)(2,1)S(1)}, bf16[96,2176]{1,0:T(8,128)(2,1)S(1)}, u32[]{:S(2)}, u32[]{:S(2)}) collective-permute-start(bf16[96,2176]{1,0:T(8,128)(2,1)S(1)} %pad_maximum_fusion), channel_id=1, source_target_pairs={{0,224},{32,0},{64,32},{96,64},{128,96},{160,128},{192,160},{224,1... | collective-permute-start | bytes 1253384 | tf_op jit(solution)/shard_map/ppermute | solution.py:255
  179.7 11.1 %collective-permute-start.17 = (bf16[96,2176]{1,0:T(8,128)(2,1)S(1)}, bf16[96,2176]{1,0:T(8,128)(2,1)S(1)}, u32[]{:S(2)}, u32[]{:S(2)}) collective-permute-start(bf16[96,2176]{1,0:T(8,128)(2,1)S(1)} %add_convert_fusion.1), channel_id=1, source_target_pairs={{0,32},{32,64},{64,96},{96,128},{128,160},{160,192},{192,224},{224... | collective-permute-start | bytes 1253384 | tf_op jit(solution)/shard_map/ppermute | solution.py:255
  182.2 17.0 %copy-start.1 = (bf16[208,2048]{1,0:T(8,128)(2,1)S(1)}, bf16[208,2048]{1,0:T(8,128)(2,1)}, u32[]{:S(2)}) copy-start(bf16[208,2048]{1,0:T(8,128)(2,1)} %copy-done) | copy-start | bytes 2555908
  182.2 11.3 %collective-permute-start.13 = (bf16[96,2176]{1,0:T(8,128)(2,1)S(1)}, bf16[96,2176]{1,0:T(8,128)(2,1)S(1)}, u32[]{:S(2)}, u32[]{:S(2)}) collective-permute-start(bf16[96,2176]{1,0:T(8,128)(2,1)S(1)} %add_convert_fusion.3), channel_id=1, source_target_pairs={{0,224},{32,0},{64,32},{96,64},{128,96},{160,128},{192,160},{224,1... | collective-permute-start | bytes 1253384 | tf_op jit(solution)/shard_map/ppermute | solution.py:255
  190.9 12.7 %collective-permute-start.18 = (bf16[96,2176]{1,0:T(8,128)(2,1)S(1)}, bf16[96,2176]{1,0:T(8,128)(2,1)S(1)}, u32[]{:S(2)}, u32[]{:S(2)}) collective-permute-start(bf16[96,2176]{1,0:T(8,128)(2,1)S(1)} %add_convert_fusion), channel_id=1, source_target_pairs={{0,32},{32,64},{64,96},{96,128},{128,160},{160,192},{192,224},{224... | collective-permute-start | bytes 1253384 | tf_op jit(solution)/shard_map/ppermute | solution.py:255
  193.6 11.2 %collective-permute-start.14 = (bf16[96,2176]{1,0:T(8,128)(2,1)S(1)}, bf16[96,2176]{1,0:T(8,128)(2,1)S(1)}, u32[]{:S(2)}, u32[]{:S(2)}) collective-permute-start(bf16[96,2176]{1,0:T(8,128)(2,1)S(1)} %add_convert_fusion.2), channel_id=1, source_target_pairs={{0,224},{32,0},{64,32},{96,64},{128,96},{160,128},{192,160},{224,1... | collective-permute-start | bytes 1253384 | tf_op jit(solution)/shard_map/ppermute | solution.py:255
  206.1 23.5 %all-to-all-start.1 = ((bf16[32,16,512]{2,1,0:T(8,128)(2,1)}), bf16[32,16,512]{2,1,0:T(8,128)(2,1)}, u32[]{:S(2)}, u32[]{:S(2)}) async-start(bf16[32,16,512]{2,1,0:T(8,128)(2,1)} %bitcast.46), calls=%async_computation.1 | async-start | bytes 1048576 | tf_op jit(solution)/shard_map/all_to_all | solution.py:353
  217.0 12.6 %copy-start.31 = (s32[1,128]{1,0:T(1,128)S(1)}, s32[1,128]{1,0:T(1,128)}, u32[]{:S(2)}) copy-start(s32[1,128]{1,0:T(1,128)} %ids_ref.3) | copy-start | bytes 1540
  217.0 12.6 %copy-start.33 = (s32[1,128]{1,0:T(1,128)S(1)}, s32[1,128]{1,0:T(1,128)}, u32[]{:S(2)}) copy-start(s32[1,128]{1,0:T(1,128)} %slot_ref.3) | copy-start | bytes 1540
  (35 other events, 160.4 us)

commit v2 on v1

v2 whole, which is shorter than its diff:
```python
import functools

import jax
import jax.numpy as jnp
from jax import lax
from jax.experimental import pallas as pl
from jax.experimental.pallas import tpu as pltpu
from jax.sharding import PartitionSpec as P

D = 2048
EXPERTS = 32
CAP = 3
SLOTS = EXPERTS * CAP
ENC = 64
TOK = 128
N_Y = 2
N_Z = 8
HID = 320
EPSILON = 1e-06
SCORE_SCALE = 0.125
COEFF = 0.7978845608
BF16 = jnp.bfloat16
F32 = jnp.float32
WIDE = D + 128


def dot(a, b, dims=((1,), (0,)), **kw):
    return lax.dot_general(a, b, (dims, ((), ())), preferred_element_type=F32, **kw)


def shuffle_matrix():
    row = lax.broadcasted_iota(jnp.int32, (512, 512), 0)
    col = lax.broadcasted_iota(jnp.int32, (512, 512), 1)
    return ((row // 16 == col % 32) & (row % 16 == col // 32)).astype(F32).astype(BF16)


def slot_table(target):
    rows = lax.broadcasted_iota(jnp.int32, (SLOTS, TOK), 0).astype(F32)
    return (rows == target).astype(F32).astype(BF16)


def call(kernel, ins, outs, hbm=(), scratch=(), flops=0, limit=16, name=None):
    specs = [
        pl.BlockSpec(memory_space=pltpu.MemorySpace.HBM if i in hbm else pltpu.MemorySpace.VMEM)
        for i in range(len(ins))
    ]
    n = len(ins) + len(outs) + len(scratch)

    def run(*refs):
        given, held, sems = list(refs[:n]), refs[n:-1], refs[-1]
        for k, i in enumerate(hbm):
            copy = pltpu.make_async_copy(given[i], held[k], sems.at[k])
            copy.start()
            given[i] = functools.partial(arrived, copy, held[k])
        kernel(*given)

    return pl.pallas_call(
        run if hbm else kernel,
        in_specs=specs,
        out_specs=[pl.BlockSpec(memory_space=pltpu.MemorySpace.VMEM)] * len(outs),
        out_shape=outs,
        scratch_shapes=list(scratch)
        + [pltpu.VMEM(ins[i].shape, ins[i].dtype) for i in hbm]
        + ([pltpu.SemaphoreType.DMA((len(hbm),))] if hbm else []),
        compiler_params=pltpu.CompilerParams(vmem_limit_bytes=limit * 1024 * 1024),
        cost_estimate=pl.CostEstimate(flops=flops, bytes_accessed=0, transcendentals=0),
        name=name,
    )(*ins)


def arrived(copy, ref):
    copy.wait()
    return ref


def shape(dims, dtype=BF16):
    return jax.ShapeDtypeStruct(dims, dtype)


def dispatch_kernel(
    resid_ref, grad_ref, gain_ref, ids_ref, slot_ref, logits_ref, out_ref, token_ref, rows_ref
):
    stream = resid_ref()[...].astype(F32)
    root_mean = jnp.sqrt(jnp.mean(stream * stream, axis=-1, keepdims=True) + EPSILON)
    normed_in = (stream / root_mean * gain_ref()[...]).astype(BF16)
    ids, slot = ids_ref()[...], slot_ref()[...]
    target = jnp.where(slot < CAP, slot * EXPERTS + ids, -1).astype(F32)
    logits = logits_ref()[...]
    powers = jnp.exp(logits - jnp.max(logits, axis=0, keepdims=True))
    probs = powers / jnp.sum(powers, axis=0, keepdims=True)
    onehot = (lax.broadcasted_iota(jnp.int32, (EXPERTS, TOK), 0) == ids).astype(F32)
    chosen = jnp.sum(probs * onehot, axis=0, keepdims=True)
    token_ref[:EXPERTS] = chosen * (onehot - probs)
    token_ref[EXPERTS : EXPERTS + 8] = jnp.concatenate([chosen] * 4 + [target] * 4, axis=0)
    table = slot_table(target)
    for half, source in enumerate((normed_in, grad_ref()[...])):
        picked = dot(table, source).astype(BF16)
        for part in range(8):
            for c in range(CAP):
                row = (half * 8 + part) * 32
                rows_ref[row : row + 32, c * 256 : (c + 1) * 256] = picked[
                    c * 32 : (c + 1) * 32, part * 256 : (part + 1) * 256
                ]
    out_ref[...] = dot(shuffle_matrix(), rows_ref[...]).astype(BF16)


def collect_kernel(in_ref, kv_ref, kv_other_ref, out_ref):
    rows = dot(shuffle_matrix(), in_ref[...], ((0,), (0,))).astype(BF16)
    for half in range(2):
        for part in range(8):
            for c in range(CAP):
                row = (half * 8 + part) * 32
                out_ref[
                    half * 96 + c * 32 : half * 96 + (c + 1) * 32, part * 256 : (part + 1) * 256
                ] = rows[row : row + 32, c * 256 : (c + 1) * 256]
    for i in range(8):
        out_ref[192:208, i * 128 : (i + 1) * 128] = kv_ref[i * 16 : (i + 1) * 16, :]
        out_ref[192:208, (i + 8) * 128 : (i + 9) * 128] = kv_other_ref[i * 16 : (i + 1) * 16, :]


def expert_kernel(n, split, *refs):
    pairs, weight_refs = refs[: 2 * n], refs[2 * n : 2 * n + 4]
    out_refs, kv_ref = refs[2 * n + 4 : -1], refs[-1]
    for i, ref in enumerate(pairs[n:]):
        kv_ref[i * 16 : (i + 1) * 16] = ref[ref.shape[0] - 16 :]
    if split:
        inputs, grads = pairs[0][:96], pairs[1][:96]
    else:
        inputs = jnp.concatenate([r[:96] for r in pairs[:n]], axis=0)
        grads = jnp.concatenate([r[96:192] for r in pairs[:n]], axis=0)
    total, gate = None, None
    for k in range(2):
        w_in, w_out = weight_refs[2 * k]()[...], weight_refs[2 * k + 1]()[...]
        hidden = dot(inputs, w_in, ((1,), (1,)))
        hidden_grad = dot(grads, w_out, ((1,), (1,)))
        square = hidden * hidden
        tangent = jnp.tanh(COEFF * (hidden + 0.044715 * square * hidden))
        half = 0.5 * (1.0 + tangent)
        slope = half + 0.5 * hidden * (1.0 - tangent * tangent) * COEFF * (1.0 + 0.134145 * square)
        scaled = (hidden_grad * slope).astype(BF16)
        part = dot(scaled, w_in)
        gates = jnp.sum(half * hidden * hidden_grad, axis=1, keepdims=True)
        total = part if total is None else total + part
        gate = gates if gate is None else gate + gates
    total = total.astype(BF16)
    gate = jnp.broadcast_to(gate, (gate.shape[0], 128)).astype(BF16)
    size = 48 if split else 96
    for i, out_ref in enumerate(out_refs):
        out_ref[:, :D] = total[i * size : (i + 1) * size]
        out_ref[:, D:] = gate[i * size : (i + 1) * size]


def experts(blocks, weights, split=False, name=None):
    n = 1 if split else len(blocks)
    outs = [shape((48, WIDE))] * 2 if split else [shape((96, WIDE))] * n
    outs.append(shape((16 * n, D)))
    kernel = functools.partial(expert_kernel, n, split)
    if not split:
        kernel = lambda *refs: expert_kernel(n, False, *refs[:n], *refs[:n], *refs[n:])
    return call(
        kernel,
        list(blocks) + list(weights),
        outs,
        hbm=tuple(range(len(blocks), len(blocks) + 4)),
        flops=2 * n * 96 * D * 2 * HID * 3,
        limit=12 if split else 40,
        name=name,
    )


def return_kernel(*refs):
    parts, out_ref, rows_ref = refs[:5], refs[5], refs[6]
    total = parts[0][...].astype(F32)
    for ref in parts[1:]:
        total = total + ref[...].astype(F32)
    total = total.astype(BF16)
    rows_ref[:, 384:] = jnp.zeros((512, 128), BF16)
    for c in range(CAP):
        for part in range(16):
            rows_ref[part * 32 : (part + 1) * 32, c * 128 : (c + 1) * 128] = total[
                c * 32 : (c + 1) * 32, part * 128 : (part + 1) * 128
            ]
        rows_ref[c * 32 : (c + 1) * 32, 384:] = total[c * 32 : (c + 1) * 32, D:]
    out_ref[...] = dot(shuffle_matrix(), rows_ref[...]).astype(BF16)


def stream_kernel(
    in_ref, token_ref, probs_ref, values_ref, weight_ref, resid_ref, gain_ref, grad_ref, query_ref,
    out_ref, terms_ref, rows_ref,
):
    rows = dot(shuffle_matrix(), in_ref[...], ((0,), (0,))).astype(BF16)
    for c in range(CAP):
        for part in range(16):
            rows_ref[c * 32 : (c + 1) * 32, part * 128 : (part + 1) * 128] = rows[
                part * 32 : (part + 1) * 32, c * 128 : (c + 1) * 128
            ]
        rows_ref[c * 32 : (c + 1) * 32, D:] = rows[c * 32 : (c + 1) * 32, 384:]
    chosen, target = token_ref[EXPERTS : EXPERTS + 1], token_ref[EXPERTS + 4 : EXPERTS + 5]
    table = slot_table(target)
    fetched = dot(table, rows_ref[:, :D], ((0,), (0,)))
    prob_grad = dot(rows_ref[:, D:], table, ((0,), (0,)))[:1]
    logit_grad = prob_grad * token_ref[:EXPERTS]
    router_term = dot(
        logit_grad, weight_ref()[...].astype(F32), ((0,), (0,)), precision=lax.Precision.HIGHEST
    )
    chosen = jnp.transpose(jnp.broadcast_to(chosen, (TOK, TOK)))[:, :1]
    stream = resid_ref()[...].astype(F32)
    root_mean = jnp.sqrt(jnp.mean(stream * stream, axis=-1, keepdims=True) + EPSILON)
    normed = stream / root_mean
    normed_grad = (chosen * fetched + router_term) * gain_ref()[...]
    mean = jnp.mean(normed_grad * normed, axis=-1, keepdims=True)
    out_ref[...] = (
        grad_ref()[...].astype(F32) + (normed_grad - normed * mean) / root_mean
    ).astype(BF16)
    attend(probs_ref(), values_ref(), query_ref(), out_ref, terms_ref)


def head_mask():
    row = lax.broadcasted_iota(jnp.int32, (256, 256), 0)
    col = lax.broadcasted_iota(jnp.int32, (256, 256), 1)
    return row // ENC == col // ENC


def by_head(rows, mask):
    return jnp.where(mask, jnp.concatenate([rows.astype(F32)] * 4, axis=0), 0.0).astype(BF16)


def probs_kernel(place_ref, query_ref, *refs):
    block_refs, probs_ref, values_ref, keys_ref = refs[:2], refs[2], refs[3], refs[4]
    blocks = [(r, k * 16) for r in block_refs for k in range(r.shape[0] // 16)]
    for i, (block_ref, first) in enumerate(blocks):
        for other in range(2):
            lanes = pl.ds(pl.multiple_of(place_ref[2 * i + other] * 128, 128), 128)
            for k in range(4):
                base = (other * 8 + k) * 128
                keys_ref[k * 16 : (k + 1) * 16, lanes] = block_ref[
                    first : first + 16, base : base + 128
                ]
                values_ref[k * 16 : (k + 1) * 16, lanes] = block_ref[
                    first : first + 16, base + 512 : base + 640
                ]
    mask = head_mask()
    query_ref = query_ref()
    for g in range(8):
        cols = slice(g * 256, (g + 1) * 256)
        scores = dot(by_head(keys_ref[:, cols], mask), query_ref[:, cols], ((1,), (1,)))
        scores = (scores * SCORE_SCALE).reshape(4, ENC, TOK)
        powers = jnp.exp(scores - jnp.max(scores, axis=1, keepdims=True))
        probs = powers / jnp.sum(powers, axis=1, keepdims=True)
        probs_ref[g] = probs.reshape(256, TOK)


def attend(probs_ref, values_ref, query_ref, stream_ref, out_ref):
    mask = head_mask()
    for g in range(8):
        cols = slice(g * 256, (g + 1) * 256)
        probs = probs_ref[g]
        context, query = stream_ref[:, cols], query_ref[:, cols]
        prob_grads = dot(by_head(values_ref[:, cols], mask), context, ((1,), (1,)))
        delta = jnp.sum((probs * prob_grads).reshape(4, ENC, TOK), axis=1, keepdims=True)
        delta = jnp.broadcast_to(delta, (4, ENC, TOK)).reshape(256, TOK)
        score_weights = (probs * (prob_grads - delta)).astype(BF16)
        key_terms = jnp.where(mask, dot(score_weights, query), 0.0)
        value_terms = jnp.where(mask, dot(probs.astype(BF16), context), 0.0)
        key_terms = jnp.sum(key_terms.reshape(4, ENC, 256), axis=0) * SCORE_SCALE
        value_terms = jnp.sum(value_terms.reshape(4, ENC, 256), axis=0)
        for half in range(2):
            row = (2 * g + half) * 128
            lanes = slice(half * 128, (half + 1) * 128)
            out_ref[row : row + 64] = key_terms[:, lanes].astype(BF16)
            out_ref[row + 64 : row + 128] = value_terms[:, lanes].astype(BF16)


def shift(a, step):
    pairs = []
    for y in range(N_Y):
        for z in range(N_Z):
            for e in range(EXPERTS):
                to = (z + (step if e % 2 == 0 else -step)) % N_Z
                pairs.append(((y * N_Z + z) * EXPERTS + e, (y * N_Z + to) * EXPERTS + e))
    return lax.ppermute(a, ("seq", "exp"), pairs)


def across(a):
    return lax.ppermute(a, "seq", [(s, (s + N_Z) % (N_Y * N_Z)) for s in range(N_Y * N_Z)])


FIRST, LAST = ((0, 48), (0, 0)), ((48, 0), (0, 0))


def plus(*parts):
    return functools.reduce(jnp.add, [a.astype(F32) for a in parts]).astype(BF16)


def call_probs(places, query, blocks):
    def run(place_ref, query_ref, *refs):
        held, sem = refs[-2:]
        copy = pltpu.make_async_copy(query_ref, held, sem)
        copy.start()
        probs_kernel(place_ref, functools.partial(arrived, copy, held), *refs[:-2])

    vmem = pl.BlockSpec(memory_space=pltpu.MemorySpace.VMEM)
    return pl.pallas_call(
        run,
        in_specs=[
            pl.BlockSpec(memory_space=pltpu.MemorySpace.SMEM),
            pl.BlockSpec(memory_space=pltpu.MemorySpace.HBM),
        ]
        + [vmem] * len(blocks),
        out_specs=[vmem] * 2,
        out_shape=[shape((8, 256, TOK), F32), shape((ENC, D))],
        scratch_shapes=[
            pltpu.VMEM((ENC, D), BF16), pltpu.VMEM((TOK, D), BF16), pltpu.SemaphoreType.DMA,
        ],
        compiler_params=pltpu.CompilerParams(vmem_limit_bytes=16 * 1024 * 1024),
        cost_estimate=pl.CostEstimate(
            flops=8 * 2 * 256 * 256 * 128, bytes_accessed=0, transcendentals=0
        ),
        name="probs",
    )(places, query, *blocks)


def body(
    resid,
    norm_gain,
    router_logits,
    router_weight,
    expert_index,
    slot,
    w_in,
    w_out,
    grad_out,
    queries,
    keys,
    values,
):
    seq = lax.axis_index("seq")
    gain = norm_gain.reshape(1, D)
    stream, upstream, query = resid[0], grad_out[0], queries[0]
    kv = jnp.concatenate([keys[0], values[0]], axis=0)
    kv_other = across(kv)
    outgoing, token_rows = call(
        dispatch_kernel,
        [stream, upstream, gain, expert_index, slot, router_logits[0].T],
        [shape((512, 768)), shape((EXPERTS + 8, TOK), F32)],
        hbm=(0, 1, 2, 3, 4, 5),
        scratch=[pltpu.VMEM((512, 768), BF16)],
        flops=2 * 512 * 512 * 768,
        limit=60,
        name="dispatch",
    )
    arrived = lax.all_to_all(outgoing, "exp", 0, 0, tiled=True)
    (block,) = call(
        collect_kernel,
        [arrived, kv, kv_other],
        [shape((208, D))],
        flops=2 * 512 * 512 * 768,
        name="collect",
    )
    block, own_in, own_out = lax.optimization_barrier((block, w_in[0].T, w_out[0]))
    other_in, other_out = across(own_in), across(own_out)
    ups, downs = [block], [block]
    for k in range(3):
        ups.append(shift(ups[-1], 1))
        downs.append(shift(downs[-1], -1))
        if k == 1:
            ups[2], downs[2], other_in = lax.optimization_barrier((ups[2], downs[2], other_in))
    weights = (own_in, own_out, other_in, other_out)
    far_in = shift(ups[3][:96], 1)
    far_grad = shift(downs[3][96:], -1)
    *near, near_kv = experts(ups + downs[1:], weights, name="experts_near")
    near, far_in = lax.optimization_barrier((near, far_in))
    own, up_parts, down_parts = near[0], near[:4], near[:1] + near[4:]
    far_a, far_b, far_kv = experts([far_in, far_grad], weights, split=True, name="experts_far")

    thirds = shift(up_parts[3], -1), shift(down_parts[3], 1)
    thirds, firsts = lax.optimization_barrier((thirds, (up_parts[1], down_parts[1])))
    back = plus(up_parts[2], thirds[0], jnp.pad(shift(far_a, -2), FIRST))
    forth = plus(down_parts[2], thirds[1], jnp.pad(shift(far_b, 2), LAST))
    sums = [own, shift(back, -2), shift(forth, 2), shift(firsts[0], -1), shift(firsts[1], 1)]

    z, y = seq % N_Z, seq // N_Z
    way = 1 - 2 * (lax.axis_index("exp") % 2)
    places = []
    for step in (0, -1, -2, -3, 1, 2, 3, 4):
        at = (z + way * step + N_Z) % N_Z
        places += [y * N_Z + at, (1 - y) * N_Z + at]
    probs, all_values = call_probs(
        jnp.stack(places).astype(jnp.int32), query, [near_kv, far_kv]
    )

    (returning,) = call(
        return_kernel,
        sums,
        [shape((512, 512))],
        scratch=[pltpu.VMEM((512, 512), BF16)],
        flops=2 * 512 * 512 * 512,
        name="return",
    )
    returned = lax.all_to_all(returning, "exp", 0, 0, tiled=True)
    grad_stream, terms = call(
        stream_kernel,
        [
            returned, token_rows, probs, all_values, router_weight.T, stream, gain, upstream, query,
        ],
        [shape((TOK, D)), shape((2048, 128))],
        hbm=(2, 3, 4, 5, 6, 7, 8),
        scratch=[pltpu.VMEM((SLOTS, WIDE), BF16)],
        flops=2 * 512 * 512 * 512 + 8 * 3 * 2 * 256 * 256 * 128,
        limit=20,
        name="stream",
    )
    terms = lax.all_to_all(terms, "seq", 0, 0, tiled=True)
    totals = jnp.sum(terms.reshape(16, 2, ENC, 128).astype(F32), axis=0).astype(BF16)
    return (grad_stream[None], totals[0][None], totals[1][None])


def solution(mesh):
    in_specs = (
        P("exp", "seq", None),
        P(),
        P("exp", "seq", None),
        P(),
        P("exp", "seq"),
        P("exp", "seq"),
        P("exp", None, "seq"),
        P("exp", "seq", None),
        P("exp", "seq", None),
        P("exp", "seq", None),
        P("exp", None, "seq"),
        P("exp", None, "seq"),
    )
    out_specs = (P("exp", "seq", None), P("exp", None, "seq"), P("exp", None, "seq"))
    return jax.shard_map(body, mesh=mesh, in_specs=in_specs, out_specs=out_specs, check_vma=False)
```

time: 266 us -> 241 us (0.906)
  local copies, waits for them, and re-layouts: 25.9 us -> 3.38 us
  waiting for transfers between devices: 86.1 us -> 97.8 us
  Pallas kernels: 34.9 us -> 24.7 us
  blocking collectives: 22.4 us -> 18.1 us
    unnamed x79 -> x28, local copies, waits for them, and re-layouts: 20.1 us -> 2.62 us
    pallas_call x11 -> x7, Pallas kernels: 34.9 us -> 24.7 us  [the longest x6 23.4 us: call(): pl.pallas_call(run if hbm else kernel, in_specs=specs, out_specs=[pl.Bloc...]
    ppermute x19, waiting for transfers between devices: 72.3 us -> 80.1 us  [the longest x16 56 us: shift(): return lax.ppermute(a, ('seq', 'exp'), pairs)]
    all_to_all x1, blocking collectives: 22.4 us -> 18.1 us  [body(): terms = lax.all_to_all(terms, 'seq', 0, 0, tiled=True)]
    all_to_all x1, waiting for transfers between devices: 9.18 us -> 13.2 us  [body(): returned = lax.all_to_all(returning, 'exp', 0, 0, tiled=True)]
  transfers between devices with their start and end apart: 21 -> 21, of which waited for: 13 -> 13; matrix products, arithmetic and copies ran while one was open for 3% -> 0% of each run, Pallas kernels for 8% -> 6%
where the time goes in v2:
time: 241 us; the launch traced here: 237 us
  waiting for transfers between devices  97.8 us (41%)
  starting transfers between devices  91.6 us (38%)
  Pallas kernels  24.7 us (10%)
  blocking collectives  18.1 us (8%)
  local copies, waits for them, and re-layouts  3.38 us (1%)
    ppermute x16, starting transfers between devices, shift(): return lax.ppermute(a, ('seq', 'exp'), pairs)  67.8 us
    ppermute x16, waiting for transfers between devices, shift(): return lax.ppermute(a, ('seq', 'exp'), pairs)  56 us
    ppermute x3, waiting for transfers between devices, across(): lax.ppermute(a, 'seq', [(s, (s + N_Z) % (N_Y * N_Z)) for s in range(N_Y *...  24.1 us
    pallas_call x6, Pallas kernels, call(): pl.pallas_call(run if hbm else kernel, in_specs=specs, out_specs=[pl.Bloc...  23.4 us
    all_to_all x1, blocking collectives, body(): terms = lax.all_to_all(terms, 'seq', 0, 0, tiled=True)  18.1 us
    all_to_all x1, waiting for transfers between devices, body(): returned = lax.all_to_all(returning, 'exp', 0, 0, tiled=True)  13.2 us
    all_to_all x1, starting transfers between devices, body(): arrived = lax.all_to_all(outgoing, 'exp', 0, 0, tiled=True)  10.4 us
    all_to_all x1, starting transfers between devices, body(): returned = lax.all_to_all(returning, 'exp', 0, 0, tiled=True)  7.01 us
  transfers between devices with their start and end apart: 21, of which 13 were waited for; matrix products, arithmetic and copies ran while one was open for 0% of the time, Pallas kernels for 6%

profile of v2, /device:TPU:6, one launch (start us, length us, event | category | flops | bytes accessed | tf_op | source)
XLA Modules:
  0.0 237.2 jit_solution(15239503310755743791)
XLA Ops:
  3.9 10.4 %all-to-all-start = ((bf16[32,16,768]{2,1,0:T(8,128)(2,1)}), bf16[32,16,768]{2,1,0:T(8,128)(2,1)S(1)}, u32[]{:S(2)}, u32[]{:S(2)}) async-start(bf16[32,16,768]{2,1,0:T(8,128)(2,1)} %bitcast.58), calls=%async_computation | async-start | bytes 1572864 | tf_op jit(solution)/shard_map/all_to_all | solution.py:352
  16.9 15.0 %collective-permute-done.kv_other_ref = bf16[128,128]{1,0:T(8,128)(2,1)S(1)} collective-permute-done((bf16[128,128]{1,0:T(8,128)(2,1)S(1)}, bf16[128,128]{1,0:T(8,128)(2,1)S(1)}, u32[]{:S(2)}, u32[]{:S(2)}) %collective-permute-start) | collective-permute-done | bytes 32800 | tf_op jit(solution)/shard_map/ppermute | solution.py:285
  32.0 4.6 %all-to-all-done = bf16[32,16,768]{2,1,0:T(8,128)(2,1)S(1)} async-done(((bf16[32,16,768]{2,1,0:T(8,128)(2,1)}), bf16[32,16,768]{2,1,0:T(8,128)(2,1)S(1)}, u32[]{:S(2)}, u32[]{:S(2)}) %all-to-all-start) | async-done | bytes 786464 | tf_op jit(solution)/shard_map/all_to_all | solution.py:352
  37.2 4.3 %collective-permute-start.1 = (bf16[208,2048]{1,0:T(8,128)(2,1)S(1)}, bf16[208,2048]{1,0:T(8,128)(2,1)S(1)}, u32[]{:S(2)}, u32[]{:S(2)}) collective-permute-start(bf16[208,2048]{1,0:T(8,128)(2,1)S(1)} %collect.1.refs_0_), channel_id=1, source_target_pairs={{0,32},{1,225},{2,34},{3,227},{4,36},{5,229},{6,38},{7,231},{8,40}... | collective-permute-start | bytes 2555912 | tf_op jit(solution)/shard_map/ppermute | solution.py:281
  41.5 8.6 %collective-permute-start.3 = (bf16[208,2048]{1,0:T(8,128)(2,1)S(1)}, bf16[208,2048]{1,0:T(8,128)(2,1)S(1)}, u32[]{:S(2)}, u32[]{:S(2)}) collective-permute-start(bf16[208,2048]{1,0:T(8,128)(2,1)S(1)} %collect.1.refs_0_), channel_id=1, source_target_pairs={{0,224},{1,33},{2,226},{3,35},{4,228},{5,37},{6,230},{7,39},{8,232... | collective-permute-start | bytes 2555912 | tf_op jit(solution)/shard_map/ppermute | solution.py:281
  52.0 12.0 %collective-permute-done.1.refs_1_ = bf16[208,2048]{1,0:T(8,128)(2,1)S(1)} collective-permute-done((bf16[208,2048]{1,0:T(8,128)(2,1)S(1)}, bf16[208,2048]{1,0:T(8,128)(2,1)S(1)}, u32[]{:S(2)}, u32[]{:S(2)}) %collective-permute-start.1) | collective-permute-done | bytes 852000 | tf_op jit(solution)/shard_map/ppermute | solution.py:281
  66.4 6.2 %collective-permute-start.4 = (bf16[208,2048]{1,0:T(8,128)(2,1)S(1)}, bf16[208,2048]{1,0:T(8,128)(2,1)S(1)}, u32[]{:S(2)}, u32[]{:S(2)}) collective-permute-start(bf16[208,2048]{1,0:T(8,128)(2,1)S(1)} %collective-permute-done.3.refs_4_), channel_id=1, source_target_pairs={{0,224},{1,33},{2,226},{3,35},{4,228},{5,37},{6,230},{7,39},{8,232... | collective-permute-start | bytes 2555912 | tf_op jit(solution)/shard_map/ppermute | solution.py:281
  74.6 9.1 %collective-permute-done.5.refs_9_.refs_4_ = bf16[320,2048]{1,0:T(8,128)(2,1)S(1)} collective-permute-done((bf16[320,2048]{1,0:T(8,128)(2,1)S(1)}, bf16[320,2048]{1,0:T(8,128)(2,1)S(1)}, u32[]{:S(2)}, u32[]{:S(2)}) %collective-permute-start.5) | collective-permute-done | bytes 1310752 | tf_op jit(solution)/shard_map/ppermute | solution.py:285
  83.7 4.5 %collective-permute-done.2.refs_2_ = bf16[208,2048]{1,0:T(8,128)(2,1)S(1)} collective-permute-done((bf16[208,2048]{1,0:T(8,128)(2,1)S(1)}, bf16[208,2048]{1,0:T(8,128)(2,1)S(1)}, u32[]{:S(2)}, u32[]{:S(2)}) %collective-permute-start.2) | collective-permute-done | bytes 852000 | tf_op jit(solution)/shard_map/ppermute | solution.py:281
  90.1 6.0 %collective-permute-start.7 = (bf16[208,2048]{1,0:T(8,128)(2,1)S(1)}, bf16[208,2048]{1,0:T(8,128)(2,1)S(1)}, u32[]{:S(2)}, u32[]{:S(2)}) collective-permute-start(bf16[208,2048]{1,0:T(8,128)(2,1)S(1)} %collective-permute-done.4.refs_5_), channel_id=1, source_target_pairs={{0,224},{1,33},{2,226},{3,35},{4,228},{5,37},{6,230},{7,39},{8,232... | collective-permute-start | bytes 2555912 | tf_op jit(solution)/shard_map/ppermute | solution.py:281
  96.1 13.5 %collective-permute-done.6.refs_3_ = bf16[208,2048]{1,0:T(8,128)(2,1)S(1)} collective-permute-done((bf16[208,2048]{1,0:T(8,128)(2,1)S(1)}, bf16[208,2048]{1,0:T(8,128)(2,1)S(1)}, u32[]{:S(2)}, u32[]{:S(2)}) %collective-permute-start.6) | collective-permute-done | bytes 852000 | tf_op jit(solution)/shard_map/ppermute | solution.py:281
  113.1 5.4 %collective-permute-start.12 = (bf16[112,2048]{1,0:T(8,128)(2,1)S(1)}, bf16[112,2048]{1,0:T(8,128)(2,1)S(1)}, u32[]{:S(2)}, u32[]{:S(2)}) collective-permute-start(bf16[112,2048]{1,0:T(8,128)(2,1)S(1)} %slice.25), channel_id=1, source_target_pairs={{0,224},{1,33},{2,226},{3,35},{4,228},{5,37},{6,230},{7,39},{8,232... | collective-permute-start | bytes 1376264 | tf_op jit(solution)/shard_map/ppermute | solution.py:281
  118.5 10.0 %experts_near.1 = (bf16[96,2176]{1,0:T(8,128)(2,1)S(1)}, bf16[96,2176]{1,0:T(8,128)(2,1)S(1)}, bf16[96,2176]{1,0:T(8,128)(2,1)S(1)}, bf16[96,2176]{1,0:T(8,128)(...) custom-call(bf16[208,2048]{1,0:T(8,128)(2,1)S(1)} %collect.1.refs_0_, ...), custom_call_target="tpu_custom_call" | custom-call | flops 5284823040 | tf_op jit(solution)/shard_map/experts_near/pallas_call | solution.py:57
  137.9 5.5 %collective-permute-start.13 = (bf16[48,2176]{1,0:T(8,128)(2,1)S(1)}, bf16[48,2176]{1,0:T(8,128)(2,1)S(1)}, u32[]{:S(2)}, u32[]{:S(2)}) collective-permute-start(bf16[48,2176]{1,0:T(8,128)(2,1)S(1)} %get-tuple-element.60), channel_id=1, source_target_pairs={{0,192},{1,65},{2,194},{3,67},{4,196},{5,69},{6,198},{7,71},{8,200... | collective-permute-start | bytes 626696 | tf_op jit(solution)/shard_map/ppermute | solution.py:281
  145.3 4.9 %collective-permute-done.13 = bf16[48,2176]{1,0:T(8,128)(2,1)S(1)} collective-permute-done((bf16[48,2176]{1,0:T(8,128)(2,1)S(1)}, bf16[48,2176]{1,0:T(8,128)(2,1)S(1)}, u32[]{:S(2)}, u32[]{:S(2)}) %collective-permute-start.13) | collective-permute-done | bytes 208928 | tf_op jit(solution)/shard_map/ppermute | solution.py:281
  150.3 6.6 %collective-permute-start.14 = (bf16[96,2176]{1,0:T(8,128)(2,1)S(1)}, bf16[96,2176]{1,0:T(8,128)(2,1)S(1)}, u32[]{:S(2)}, u32[]{:S(2)}) collective-permute-start(bf16[96,2176]{1,0:T(8,128)(2,1)S(1)} %add_convert_fusion.1), channel_id=1, source_target_pairs={{0,192},{1,65},{2,194},{3,67},{4,196},{5,69},{6,198},{7,71},{8,200... | collective-permute-start | bytes 1253384 | tf_op jit(solution)/shard_map/ppermute | solution.py:281
  157.3 4.9 %collective-permute-start.16 = (bf16[96,2176]{1,0:T(8,128)(2,1)S(1)}, bf16[96,2176]{1,0:T(8,128)(2,1)S(1)}, u32[]{:S(2)}, u32[]{:S(2)}) collective-permute-start(bf16[96,2176]{1,0:T(8,128)(2,1)S(1)} %add_convert_fusion), channel_id=1, source_target_pairs={{0,64},{1,193},{2,66},{3,195},{4,68},{5,197},{6,70},{7,199},{8,72}... | collective-permute-start | bytes 1253384 | tf_op jit(solution)/shard_map/ppermute | solution.py:281
  162.2 4.6 %collective-permute-start.17 = (bf16[96,2176]{1,0:T(8,128)(2,1)S(1)}, bf16[96,2176]{1,0:T(8,128)(2,1)S(1)}, u32[]{:S(2)}, u32[]{:S(2)}) collective-permute-start(bf16[96,2176]{1,0:T(8,128)(2,1)S(1)} %get-tuple-element.64), channel_id=1, source_target_pairs={{0,224},{1,33},{2,226},{3,35},{4,228},{5,37},{6,230},{7,39},{8,232... | collective-permute-start | bytes 1253384 | tf_op jit(solution)/shard_map/ppermute | solution.py:281
  168.8 9.7 %collective-permute-done.14.refs_1_ = bf16[96,2176]{1,0:T(8,128)(2,1)S(1)} collective-permute-done((bf16[96,2176]{1,0:T(8,128)(2,1)S(1)}, bf16[96,2176]{1,0:T(8,128)(2,1)S(1)}, u32[]{:S(2)}, u32[]{:S(2)}) %collective-permute-start.14) | collective-permute-done | bytes 417824 | tf_op jit(solution)/shard_map/ppermute | solution.py:281
  178.5 9.2 %collective-permute-done.17.refs_3_ = bf16[96,2176]{1,0:T(8,128)(2,1)S(1)} collective-permute-done((bf16[96,2176]{1,0:T(8,128)(2,1)S(1)}, bf16[96,2176]{1,0:T(8,128)(2,1)S(1)}, u32[]{:S(2)}, u32[]{:S(2)}) %collective-permute-start.17) | collective-permute-done | bytes 417824 | tf_op jit(solution)/shard_map/ppermute | solution.py:281
  189.2 7.0 %all-to-all-start.1 = ((bf16[32,16,512]{2,1,0:T(8,128)(2,1)}), bf16[32,16,512]{2,1,0:T(8,128)(2,1)S(1)}, u32[]{:S(2)}, u32[]{:S(2)}) async-start(bf16[32,16,512]{2,1,0:T(8,128)(2,1)} %bitcast.12), calls=%async_computation.1 | async-start | bytes 1048576 | tf_op jit(solution)/shard_map/all_to_all | solution.py:400
  199.7 13.2 %all-to-all-done.1 = bf16[32,16,512]{2,1,0:T(8,128)(2,1)S(1)} async-done(((bf16[32,16,512]{2,1,0:T(8,128)(2,1)}), bf16[32,16,512]{2,1,0:T(8,128)(2,1)S(1)}, u32[]{:S(2)}, u32[]{:S(2)}) %all-to-all-start.1) | async-done | bytes 524320 | tf_op jit(solution)/shard_map/all_to_all | solution.py:400
  213.6 4.8 %stream.1 = (bf16[128,2048]{1,0:T(8,128)(2,1)}, bf16[2048,128]{1,0:T(8,128)(2,1)S(1)}) custom-call(bf16[512,512]{1,0:T(8,128)(2,1)S(1)} %bitcast.41, f32[40,128]{1,0:T(8,128)S(1)} %copy-done.10, f32[8,256,128]{2,1,0:T(8,128)S(1)} %get-tuple-element.69.refs_2_, bf16[64,2048]{1,0:T(8,128)(2,1)S(1)} %get-tuple-element.70.refs_3_, ...), custom_call_target="tpu_custom_call" | custom-call | flops 671088640 | tf_op jit(solution)/shard_map/stream/pallas_call | solution.py:57
  218.4 18.1 %all_to_all.31 = bf16[16,128,128]{2,1,0:T(8,128)(2,1)S(1)} all-to-all(bf16[16,128,128]{2,1,0:T(8,128)(2,1)S(1)} %bitcast.50), channel_id=1, replica_groups=mesh['seq'=16,'exp'=32] {'seq'}, dimensions={0} | all-to-all | bytes 1048576 | tf_op jit(solution)/shard_map/all_to_all | solution.py:413
  (62 shorter events, 37.8 us)
Async XLA Ops:
  3.9 46.2 %copy-start.1 = (bf16[1,2048,320]{1,2,0:T(8,128)(2,1)S(1)}, bf16[1,2048,320]{1,2,0:T(8,128)(2,1)}, u32[]{:S(2)}) copy-start(bf16[1,2048,320]{1,2,0:T(8,128)(2,1)} %param.18) | copy-start | bytes 3932164
  3.9 68.8 %copy-start.2 = (bf16[1,320,2048]{2,1,0:T(8,128)(2,1)S(1)}, bf16[1,320,2048]{2,1,0:T(8,128)(2,1)}, u32[]{:S(2)}) copy-start(bf16[1,320,2048]{2,1,0:T(8,128)(2,1)} %param.19) | copy-start | bytes 3932164
  3.9 32.6 %all-to-all-start = ((bf16[32,16,768]{2,1,0:T(8,128)(2,1)}), bf16[32,16,768]{2,1,0:T(8,128)(2,1)S(1)}, u32[]{:S(2)}, u32[]{:S(2)}) async-start(bf16[32,16,768]{2,1,0:T(8,128)(2,1)} %bitcast.58), calls=%async_computation | async-start | bytes 1572864 | tf_op jit(solution)/shard_map/all_to_all | solution.py:352
  14.3 17.6 %collective-permute-start = (bf16[128,128]{1,0:T(8,128)(2,1)S(1)}, bf16[128,128]{1,0:T(8,128)(2,1)S(1)}, u32[]{:S(2)}, u32[]{:S(2)}) collective-permute-start(bf16[128,128]{1,0:T(8,128)(2,1)S(1)} %pad_maximum_fusion.kv_ref), channel_id=1, source_target_pairs={{0,256},{32,288},{64,320},{96,352},{128,384},{160,416},{192,448},{... | collective-permute-start | bytes 98312 | tf_op jit(solution)/shard_map/ppermute | solution.py:285
  37.2 26.9 %collective-permute-start.1 = (bf16[208,2048]{1,0:T(8,128)(2,1)S(1)}, bf16[208,2048]{1,0:T(8,128)(2,1)S(1)}, u32[]{:S(2)}, u32[]{:S(2)}) collective-permute-start(bf16[208,2048]{1,0:T(8,128)(2,1)S(1)} %collect.1.refs_0_), channel_id=1, source_target_pairs={{0,32},{1,225},{2,34},{3,227},{4,36},{5,229},{6,38},{7,231},{8,40}... | collective-permute-start | bytes 2555912 | tf_op jit(solution)/shard_map/ppermute | solution.py:281
  41.5 24.9 %collective-permute-start.3 = (bf16[208,2048]{1,0:T(8,128)(2,1)S(1)}, bf16[208,2048]{1,0:T(8,128)(2,1)S(1)}, u32[]{:S(2)}, u32[]{:S(2)}) collective-permute-start(bf16[208,2048]{1,0:T(8,128)(2,1)S(1)} %collect.1.refs_0_), channel_id=1, source_target_pairs={{0,224},{1,33},{2,226},{3,35},{4,228},{5,37},{6,230},{7,39},{8,232... | collective-permute-start | bytes 2555912 | tf_op jit(solution)/shard_map/ppermute | solution.py:281
  50.1 33.6 %collective-permute-start.5 = (bf16[320,2048]{1,0:T(8,128)(2,1)S(1)}, bf16[320,2048]{1,0:T(8,128)(2,1)S(1)}, u32[]{:S(2)}, u32[]{:S(2)}) collective-permute-start(bf16[320,2048]{1,0:T(8,128)(2,1)S(1)} %bitcast.44), channel_id=1, source_target_pairs={{0,256},{32,288},{64,320},{96,352},{128,384},{160,416},{192,448},{... | collective-permute-start | bytes 3932168 | tf_op jit(solution)/shard_map/ppermute | solution.py:285
  64.1 24.1 %collective-permute-start.2 = (bf16[208,2048]{1,0:T(8,128)(2,1)S(1)}, bf16[208,2048]{1,0:T(8,128)(2,1)S(1)}, u32[]{:S(2)}, u32[]{:S(2)}) collective-permute-start(bf16[208,2048]{1,0:T(8,128)(2,1)S(1)} %collective-permute-done.1.refs_1_), channel_id=1, source_target_pairs={{0,32},{1,225},{2,34},{3,227},{4,36},{5,229},{6,38},{7,231},{8,40}... | collective-permute-start | bytes 2555912 | tf_op jit(solution)/shard_map/ppermute | solution.py:281
  66.4 21.7 %collective-permute-start.4 = (bf16[208,2048]{1,0:T(8,128)(2,1)S(1)}, bf16[208,2048]{1,0:T(8,128)(2,1)S(1)}, u32[]{:S(2)}, u32[]{:S(2)}) collective-permute-start(bf16[208,2048]{1,0:T(8,128)(2,1)S(1)} %collective-permute-done.3.refs_4_), channel_id=1, source_target_pairs={{0,224},{1,33},{2,226},{3,35},{4,228},{5,37},{6,230},{7,39},{8,232... | collective-permute-start | bytes 2555912 | tf_op jit(solution)/shard_map/ppermute | solution.py:281
  72.7 45.9 %collective-permute-start.8 = (bf16[320,2048]{1,0:T(8,128)(2,1)S(1)}, bf16[320,2048]{1,0:T(8,128)(2,1)S(1)}, u32[]{:S(2)}, u32[]{:S(2)}) collective-permute-start(bf16[320,2048]{1,0:T(8,128)(2,1)S(1)} %bitcast.47), channel_id=1, source_target_pairs={{0,256},{32,288},{64,320},{96,352},{128,384},{160,416},{192,448},{... | collective-permute-start | bytes 3932168 | tf_op jit(solution)/shard_map/ppermute | solution.py:285
  88.2 21.4 %collective-permute-start.6 = (bf16[208,2048]{1,0:T(8,128)(2,1)S(1)}, bf16[208,2048]{1,0:T(8,128)(2,1)S(1)}, u32[]{:S(2)}, u32[]{:S(2)}) collective-permute-start(bf16[208,2048]{1,0:T(8,128)(2,1)S(1)} %collective-permute-done.2.refs_2_), channel_id=1, source_target_pairs={{0,32},{1,225},{2,34},{3,227},{4,36},{5,229},{6,38},{7,231},{8,40}... | collective-permute-start | bytes 2555912 | tf_op jit(solution)/shard_map/ppermute | solution.py:281
  90.1 23.0 %collective-permute-start.7 = (bf16[208,2048]{1,0:T(8,128)(2,1)S(1)}, bf16[208,2048]{1,0:T(8,128)(2,1)S(1)}, u32[]{:S(2)}, u32[]{:S(2)}) collective-permute-start(bf16[208,2048]{1,0:T(8,128)(2,1)S(1)} %collective-permute-done.4.refs_5_), channel_id=1, source_target_pairs={{0,224},{1,33},{2,226},{3,35},{4,228},{5,37},{6,230},{7,39},{8,232... | collective-permute-start | bytes 2555912 | tf_op jit(solution)/shard_map/ppermute | solution.py:281
  109.6 18.9 %collective-permute-start.9 = (bf16[96,2048]{1,0:T(8,128)(2,1)S(1)}, bf16[96,2048]{1,0:T(8,128)(2,1)S(1)}, u32[]{:S(2)}, u32[]{:S(2)}) collective-permute-start(bf16[96,2048]{1,0:T(8,128)(2,1)S(1)} %slice.24), channel_id=1, source_target_pairs={{0,32},{1,225},{2,34},{3,227},{4,36},{5,229},{6,38},{7,231},{8,40}... | collective-permute-start | bytes 1179656 | tf_op jit(solution)/shard_map/ppermute | solution.py:281
  113.1 21.5 %collective-permute-start.12 = (bf16[112,2048]{1,0:T(8,128)(2,1)S(1)}, bf16[112,2048]{1,0:T(8,128)(2,1)S(1)}, u32[]{:S(2)}, u32[]{:S(2)}) collective-permute-start(bf16[112,2048]{1,0:T(8,128)(2,1)S(1)} %slice.25), channel_id=1, source_target_pairs={{0,224},{1,33},{2,226},{3,35},{4,228},{5,37},{6,230},{7,39},{8,232... | collective-permute-start | bytes 1376264 | tf_op jit(solution)/shard_map/ppermute | solution.py:281
  128.5 16.7 %collective-permute-start.10 = (bf16[96,2176]{1,0:T(8,128)(2,1)S(1)}, bf16[96,2176]{1,0:T(8,128)(2,1)S(1)}, u32[]{:S(2)}, u32[]{:S(2)}) collective-permute-start(bf16[96,2176]{1,0:T(8,128)(2,1)S(1)} %get-tuple-element.54), channel_id=1, source_target_pairs={{0,224},{1,33},{2,226},{3,35},{4,228},{5,37},{6,230},{7,39},{8,232... | collective-permute-start | bytes 1253384 | tf_op jit(solution)/shard_map/ppermute | solution.py:281
  132.1 13.2 %collective-permute-start.11 = (bf16[96,2176]{1,0:T(8,128)(2,1)S(1)}, bf16[96,2176]{1,0:T(8,128)(2,1)S(1)}, u32[]{:S(2)}, u32[]{:S(2)}) collective-permute-start(bf16[96,2176]{1,0:T(8,128)(2,1)S(1)} %get-tuple-element.55), channel_id=1, source_target_pairs={{0,32},{1,225},{2,34},{3,227},{4,36},{5,229},{6,38},{7,231},{8,40}... | collective-permute-start | bytes 1253384 | tf_op jit(solution)/shard_map/ppermute | solution.py:281
  137.9 12.3 %collective-permute-start.13 = (bf16[48,2176]{1,0:T(8,128)(2,1)S(1)}, bf16[48,2176]{1,0:T(8,128)(2,1)S(1)}, u32[]{:S(2)}, u32[]{:S(2)}) collective-permute-start(bf16[48,2176]{1,0:T(8,128)(2,1)S(1)} %get-tuple-element.60), channel_id=1, source_target_pairs={{0,192},{1,65},{2,194},{3,67},{4,196},{5,69},{6,198},{7,71},{8,200... | collective-permute-start | bytes 626696 | tf_op jit(solution)/shard_map/ppermute | solution.py:281
  143.3 13.7 %collective-permute-start.15 = (bf16[48,2176]{1,0:T(8,128)(2,1)S(1)}, bf16[48,2176]{1,0:T(8,128)(2,1)S(1)}, u32[]{:S(2)}, u32[]{:S(2)}) collective-permute-start(bf16[48,2176]{1,0:T(8,128)(2,1)S(1)} %get-tuple-element.63), channel_id=1, source_target_pairs={{0,64},{1,193},{2,66},{3,195},{4,68},{5,197},{6,70},{7,199},{8,72}... | collective-permute-start | bytes 626696 | tf_op jit(solution)/shard_map/ppermute | solution.py:281
  150.3 28.1 %collective-permute-start.14 = (bf16[96,2176]{1,0:T(8,128)(2,1)S(1)}, bf16[96,2176]{1,0:T(8,128)(2,1)S(1)}, u32[]{:S(2)}, u32[]{:S(2)}) collective-permute-start(bf16[96,2176]{1,0:T(8,128)(2,1)S(1)} %add_convert_fusion.1), channel_id=1, source_target_pairs={{0,192},{1,65},{2,194},{3,67},{4,196},{5,69},{6,198},{7,71},{8,200... | collective-permute-start | bytes 1253384 | tf_op jit(solution)/shard_map/ppermute | solution.py:281
  157.3 21.2 %collective-permute-start.16 = (bf16[96,2176]{1,0:T(8,128)(2,1)S(1)}, bf16[96,2176]{1,0:T(8,128)(2,1)S(1)}, u32[]{:S(2)}, u32[]{:S(2)}) collective-permute-start(bf16[96,2176]{1,0:T(8,128)(2,1)S(1)} %add_convert_fusion), channel_id=1, source_target_pairs={{0,64},{1,193},{2,66},{3,195},{4,68},{5,197},{6,70},{7,199},{8,72}... | collective-permute-start | bytes 1253384 | tf_op jit(solution)/shard_map/ppermute | solution.py:281
  162.2 25.5 %collective-permute-start.17 = (bf16[96,2176]{1,0:T(8,128)(2,1)S(1)}, bf16[96,2176]{1,0:T(8,128)(2,1)S(1)}, u32[]{:S(2)}, u32[]{:S(2)}) collective-permute-start(bf16[96,2176]{1,0:T(8,128)(2,1)S(1)} %get-tuple-element.64), channel_id=1, source_target_pairs={{0,224},{1,33},{2,226},{3,35},{4,228},{5,37},{6,230},{7,39},{8,232... | collective-permute-start | bytes 1253384 | tf_op jit(solution)/shard_map/ppermute | solution.py:281
  166.8 20.9 %collective-permute-start.18 = (bf16[96,2176]{1,0:T(8,128)(2,1)S(1)}, bf16[96,2176]{1,0:T(8,128)(2,1)S(1)}, u32[]{:S(2)}, u32[]{:S(2)}) collective-permute-start(bf16[96,2176]{1,0:T(8,128)(2,1)S(1)} %get-tuple-element.65), channel_id=1, source_target_pairs={{0,32},{1,225},{2,34},{3,227},{4,36},{5,229},{6,38},{7,231},{8,40}... | collective-permute-start | bytes 1253384 | tf_op jit(solution)/shard_map/ppermute | solution.py:281
  187.7 25.2 %copy-start.11 = (f32[2048]{0:T(1024)S(1)}, f32[2048]{0:T(1024)}, u32[]{:S(2)}) copy-start(f32[2048]{0:T(1024)} %param.13) | copy-start | bytes 24580
  189.2 23.6 %all-to-all-start.1 = ((bf16[32,16,512]{2,1,0:T(8,128)(2,1)}), bf16[32,16,512]{2,1,0:T(8,128)(2,1)S(1)}, u32[]{:S(2)}, u32[]{:S(2)}) async-start(bf16[32,16,512]{2,1,0:T(8,128)(2,1)} %bitcast.12), calls=%async_computation.1 | async-start | bytes 1048576 | tf_op jit(solution)/shard_map/all_to_all | solution.py:400
  (11 other events, 138.4 us)

commit v3 on v2

--- a/solution.py
+++ b/solution.py
@@ -28,10 +28,10 @@
     return lax.dot_general(a, b, (dims, ((), ())), preferred_element_type=F32, **kw)
 
 
-def shuffle_matrix():
-    row = lax.broadcasted_iota(jnp.int32, (512, 512), 0)
-    col = lax.broadcasted_iota(jnp.int32, (512, 512), 1)
-    return ((row // 16 == col % 32) & (row % 16 == col // 32)).astype(F32).astype(BF16)
+def shuffle_matrix(parts):
+    row = lax.broadcasted_iota(jnp.int32, (32 * parts, 32 * parts), 0)
+    col = lax.broadcasted_iota(jnp.int32, (32 * parts, 32 * parts), 1)
+    return ((row // parts == col % 32) & (row % parts == col // 32)).astype(F32).astype(BF16)
 
 
 def slot_table(target):
@@ -101,11 +101,11 @@
                 rows_ref[row : row + 32, c * 256 : (c + 1) * 256] = picked[
                     c * 32 : (c + 1) * 32, part * 256 : (part + 1) * 256
                 ]
-    out_ref[...] = dot(shuffle_matrix(), rows_ref[...]).astype(BF16)
+    out_ref[...] = dot(shuffle_matrix(16), rows_ref[...]).astype(BF16)
 
 
 def collect_kernel(in_ref, kv_ref, kv_other_ref, out_ref):
-    rows = dot(shuffle_matrix(), in_ref[...], ((0,), (0,))).astype(BF16)
+    rows = dot(shuffle_matrix(16), in_ref[...], ((0,), (0,))).astype(BF16)
     for half in range(2):
         for part in range(8):
             for c in range(CAP):
@@ -169,32 +169,33 @@
 
 
 def return_kernel(*refs):
-    parts, out_ref, rows_ref = refs[:5], refs[5], refs[6]
+    parts, out_ref, rows_ref = refs[:3], refs[3], refs[4]
     total = parts[0][...].astype(F32)
     for ref in parts[1:]:
         total = total + ref[...].astype(F32)
     total = total.astype(BF16)
-    rows_ref[:, 384:] = jnp.zeros((512, 128), BF16)
+    rows_ref[:, 768:] = jnp.zeros((256, 128), BF16)
     for c in range(CAP):
-        for part in range(16):
-            rows_ref[part * 32 : (part + 1) * 32, c * 128 : (c + 1) * 128] = total[
-                c * 32 : (c + 1) * 32, part * 128 : (part + 1) * 128
+        for part in range(8):
+            rows_ref[part * 32 : (part + 1) * 32, c * 256 : (c + 1) * 256] = total[
+                c * 32 : (c + 1) * 32, part * 256 : (part + 1) * 256
             ]
-        rows_ref[c * 32 : (c + 1) * 32, 384:] = total[c * 32 : (c + 1) * 32, D:]
-    out_ref[...] = dot(shuffle_matrix(), rows_ref[...]).astype(BF16)
+        rows_ref[c * 32 : (c + 1) * 32, 768:] = total[c * 32 : (c + 1) * 32, D:]
+    out_ref[...] = dot(shuffle_matrix(8), rows_ref[...]).astype(BF16)
 
 
 def stream_kernel(
-    in_ref, token_ref, probs_ref, values_ref, weight_ref, resid_ref, gain_ref, grad_ref, query_ref,
+    in_ref, token_ref, probs_ref, weight_ref, resid_ref, gain_ref, grad_ref, query_ref,
     out_ref, terms_ref, rows_ref,
 ):
-    rows = dot(shuffle_matrix(), in_ref[...], ((0,), (0,))).astype(BF16)
+    rows = dot(shuffle_matrix(8), in_ref[...], ((0,), (0,))).astype(BF16)
     for c in range(CAP):
-        for part in range(16):
-            rows_ref[c * 32 : (c + 1) * 32, part * 128 : (part + 1) * 128] = rows[
-                part * 32 : (part + 1) * 32, c * 128 : (c + 1) * 128
+        for part in range(8):
+            rows_ref[c * 32 : (c + 1) * 32, part * 256 : (part + 1) * 256] = rows[
+                part * 32 : (part + 1) * 32, c * 256 : (c + 1) * 256
             ]
-        rows_ref[c * 32 : (c + 1) * 32, D:] = rows[c * 32 : (c + 1) * 32, 384:]
+        rows_ref[c * 32 : (c + 1) * 32, D:] = rows[c * 32 : (c + 1) * 32, 768:]
+    token_ref = token_ref()
     chosen, target = token_ref[EXPERTS : EXPERTS + 1], token_ref[EXPERTS + 4 : EXPERTS + 5]
     table = slot_table(target)
     fetched = dot(table, rows_ref[:, :D], ((0,), (0,)))
@@ -212,7 +213,7 @@
     out_ref[...] = (
         grad_ref()[...].astype(F32) + (normed_grad - normed * mean) / root_mean
     ).astype(BF16)
-    attend(probs_ref(), values_ref(), query_ref(), out_ref, terms_ref)
+    attend(probs_ref(), query_ref(), out_ref, terms_ref)
 
 
 def head_mask():
@@ -226,7 +227,7 @@
 
 
 def probs_kernel(place_ref, query_ref, *refs):
-    block_refs, probs_ref, values_ref, keys_ref = refs[:2], refs[2], refs[3], refs[4]
+    block_refs, probs_ref, values_ref, keys_ref = refs[:3], refs[3], refs[4], refs[5]
     blocks = [(r, k * 16) for r in block_refs for k in range(r.shape[0] // 16)]
     for i, (block_ref, first) in enumerate(blocks):
         for other in range(2):
@@ -247,16 +248,22 @@
         scores = (scores * SCORE_SCALE).reshape(4, ENC, TOK)
         powers = jnp.exp(scores - jnp.max(scores, axis=1, keepdims=True))
         probs = powers / jnp.sum(powers, axis=1, keepdims=True)
-        probs_ref[g] = probs.reshape(256, TOK)
-
-
-def attend(probs_ref, values_ref, query_ref, stream_ref, out_ref):
+        probs_ref[g, :256] = probs.reshape(256, TOK)
+        for half in range(2):
+            lanes = slice(g * 256 + half * 128, g * 256 + (half + 1) * 128)
+            probs_ref[g, 256 + half * ENC : 256 + (half + 1) * ENC] = values_ref[:, lanes].astype(F32)
+
+
+def attend(probs_ref, query_ref, stream_ref, out_ref):
     mask = head_mask()
     for g in range(8):
         cols = slice(g * 256, (g + 1) * 256)
-        probs = probs_ref[g]
+        probs = probs_ref[g, :256]
+        values = jnp.concatenate(
+            [probs_ref[g, 256 : 256 + ENC], probs_ref[g, 256 + ENC :]], axis=1
+        )
         context, query = stream_ref[:, cols], query_ref[:, cols]
-        prob_grads = dot(by_head(values_ref[:, cols], mask), context, ((1,), (1,)))
+        prob_grads = dot(by_head(values, mask), context, ((1,), (1,)))
         delta = jnp.sum((probs * prob_grads).reshape(4, ENC, TOK), axis=1, keepdims=True)
         delta = jnp.broadcast_to(delta, (4, ENC, TOK)).reshape(256, TOK)
         score_weights = (probs * (prob_grads - delta)).astype(BF16)
@@ -307,10 +314,11 @@
             pl.BlockSpec(memory_space=pltpu.MemorySpace.HBM),
         ]
         + [vmem] * len(blocks),
-        out_specs=[vmem] * 2,
-        out_shape=[shape((8, 256, TOK), F32), shape((ENC, D))],
+        out_specs=[vmem],
+        out_shape=[shape((8, 384, TOK), F32)],
         scratch_shapes=[
-            pltpu.VMEM((ENC, D), BF16), pltpu.VMEM((TOK, D), BF16), pltpu.SemaphoreType.DMA,
+            pltpu.VMEM((ENC, D), BF16), pltpu.VMEM((ENC, D), BF16), pltpu.VMEM((TOK, D), BF16),
+            pltpu.SemaphoreType.DMA,
         ],
         compiler_params=pltpu.CompilerParams(vmem_limit_bytes=16 * 1024 * 1024),
         cost_estimate=pl.CostEstimate(
@@ -368,43 +376,45 @@
     weights = (own_in, own_out, other_in, other_out)
     far_in = shift(ups[3][:96], 1)
     far_grad = shift(downs[3][96:], -1)
-    *near, near_kv = experts(ups + downs[1:], weights, name="experts_near")
-    near, far_in = lax.optimization_barrier((near, far_in))
-    own, up_parts, down_parts = near[0], near[:4], near[:1] + near[4:]
+    up_3, down_3, third_kv = experts([ups[3], downs[3]], weights, name="experts_third")
+    up_3, down_3, far_in = lax.optimization_barrier((up_3, down_3, far_in))
     far_a, far_b, far_kv = experts([far_in, far_grad], weights, split=True, name="experts_far")
-
-    thirds = shift(up_parts[3], -1), shift(down_parts[3], 1)
-    thirds, firsts = lax.optimization_barrier((thirds, (up_parts[1], down_parts[1])))
-    back = plus(up_parts[2], thirds[0], jnp.pad(shift(far_a, -2), FIRST))
-    forth = plus(down_parts[2], thirds[1], jnp.pad(shift(far_b, 2), LAST))
-    sums = [own, shift(back, -2), shift(forth, 2), shift(firsts[0], -1), shift(firsts[1], 1)]
+    far_a, far_b, block = lax.optimization_barrier((far_a, far_b, block))
+    *near, near_kv = experts([block, *ups[1:3], *downs[1:3]], weights, name="experts_near")
+    own, up_parts, down_parts = near[0], near[:3], near[:1] + near[3:]
+
+    back = plus(up_parts[2], shift(up_3, -1), jnp.pad(shift(far_a, -2), FIRST))
+    forth = plus(down_parts[2], shift(down_3, 1), jnp.pad(shift(far_b, 2), LAST))
+    back = plus(up_parts[1], shift(back, -1))
+    forth = plus(down_parts[1], shift(forth, 1))
+    sums = [own, shift(back, -1), shift(forth, 1)]
 
     z, y = seq % N_Z, seq // N_Z
     way = 1 - 2 * (lax.axis_index("exp") % 2)
     places = []
-    for step in (0, -1, -2, -3, 1, 2, 3, 4):
+    for step in (0, -1, -2, 1, 2, -3, 3, 4):
         at = (z + way * step + N_Z) % N_Z
         places += [y * N_Z + at, (1 - y) * N_Z + at]
-    probs, all_values = call_probs(
-        jnp.stack(places).astype(jnp.int32), query, [near_kv, far_kv]
+    (probs,) = call_probs(
+        jnp.stack(places).astype(jnp.int32), query, [near_kv, third_kv, far_kv]
     )
 
     (returning,) = call(
         return_kernel,
         sums,
-        [shape((512, 512))],
-        scratch=[pltpu.VMEM((512, 512), BF16)],
-        flops=2 * 512 * 512 * 512,
+        [shape((256, 896))],
+        scratch=[pltpu.VMEM((256, 896), BF16)],
+        flops=2 * 256 * 256 * 896,
         name="return",
     )
     returned = lax.all_to_all(returning, "exp", 0, 0, tiled=True)
     grad_stream, terms = call(
         stream_kernel,
         [
-            returned, token_rows, probs, all_values, router_weight.T, stream, gain, upstream, query,
+            returned, token_rows, probs, router_weight.T, stream, gain, upstream, query,
         ],
         [shape((TOK, D)), shape((2048, 128))],
-        hbm=(2, 3, 4, 5, 6, 7, 8),
+        hbm=(1, 2, 3, 4, 5, 6, 7),
         scratch=[pltpu.VMEM((SLOTS, WIDE), BF16)],
         flops=2 * 512 * 512 * 512 + 8 * 3 * 2 * 256 * 256 * 128,
         limit=20,

time: 241 us -> 237 us (0.983)
  waiting for transfers between devices: 97.8 us -> 91.2 us
  blocking collectives: 18.1 us -> 23.4 us
  starting transfers between devices: 91.6 us -> 87.8 us
    ppermute x16, starting transfers between devices: 67.8 us -> 62.4 us  [shift(): return lax.ppermute(a, ('seq', 'exp'), pairs)]
    all_to_all x1, blocking collectives: 18.1 us -> 23.4 us  [body(): terms = lax.all_to_all(terms, 'seq', 0, 0, tiled=True)]
    ppermute x16, waiting for transfers between devices: 56 us -> 52.1 us  [shift(): return lax.ppermute(a, ('seq', 'exp'), pairs)]
    all_to_all x1, waiting for transfers between devices: 13.2 us -> 10.4 us  [body(): returned = lax.all_to_all(returning, 'exp', 0, 0, tiled=True)]
    pallas_call x6 -> x7, Pallas kernels: 23.4 us -> 24.5 us  [call(): pl.pallas_call(run if hbm else kernel, in_specs=specs, out_specs=[pl.Bloc...]
  transfers between devices with their start and end apart: 21 -> 21, of which waited for: 13 -> 12; matrix products, arithmetic and copies ran while one was open for 0% -> 0% of each run, Pallas kernels for 6% -> 7%
where the time goes in v3:
time: 237 us; the launch traced here: 234 us
  waiting for transfers between devices  91.2 us (38%)
  starting transfers between devices  87.8 us (37%)
  Pallas kernels  25.8 us (11%)
  blocking collectives  23.4 us (10%)
  local copies, waits for them, and re-layouts  4.31 us (2%)
    ppermute x16, starting transfers between devices, shift(): return lax.ppermute(a, ('seq', 'exp'), pairs)  62.4 us
    ppermute x16, waiting for transfers between devices, shift(): return lax.ppermute(a, ('seq', 'exp'), pairs)  52.1 us
    pallas_call x7, Pallas kernels, call(): pl.pallas_call(run if hbm else kernel, in_specs=specs, out_specs=[pl.Bloc...  24.5 us
    ppermute x3, waiting for transfers between devices, across(): lax.ppermute(a, 'seq', [(s, (s + N_Z) % (N_Y * N_Z)) for s in range(N_Y *...  24.1 us
    all_to_all x1, blocking collectives, body(): terms = lax.all_to_all(terms, 'seq', 0, 0, tiled=True)  23.4 us
    all_to_all x1, waiting for transfers between devices, body(): returned = lax.all_to_all(returning, 'exp', 0, 0, tiled=True)  10.4 us
    all_to_all x1, starting transfers between devices, body(): arrived = lax.all_to_all(outgoing, 'exp', 0, 0, tiled=True)  10.4 us
    all_to_all x1, starting transfers between devices, body(): returned = lax.all_to_all(returning, 'exp', 0, 0, tiled=True)  8.58 us
  transfers between devices with their start and end apart: 21, of which 12 were waited for; matrix products, arithmetic and copies ran while one was open for 0% of the time, Pallas kernels for 7%

profile of v3, /device:TPU:6, one launch (start us, length us, event | category | flops | bytes accessed | tf_op | source)
XLA Modules:
  0.0 234.2 jit_solution(6545532700437826372)
XLA Ops:
  3.9 10.4 %all-to-all-start = ((bf16[32,16,768]{2,1,0:T(8,128)(2,1)}), bf16[32,16,768]{2,1,0:T(8,128)(2,1)S(1)}, u32[]{:S(2)}, u32[]{:S(2)}) async-start(bf16[32,16,768]{2,1,0:T(8,128)(2,1)} %bitcast.60), calls=%async_computation | async-start | bytes 1572864 | tf_op jit(solution)/shard_map/all_to_all | solution.py:360
  16.9 15.0 %collective-permute-done.kv_other_ref = bf16[128,128]{1,0:T(8,128)(2,1)S(1)} collective-permute-done((bf16[128,128]{1,0:T(8,128)(2,1)S(1)}, bf16[128,128]{1,0:T(8,128)(2,1)S(1)}, u32[]{:S(2)}, u32[]{:S(2)}) %collective-permute-start) | collective-permute-done | bytes 32800 | tf_op jit(solution)/shard_map/ppermute | solution.py:292
  32.0 4.6 %all-to-all-done = bf16[32,16,768]{2,1,0:T(8,128)(2,1)S(1)} async-done(((bf16[32,16,768]{2,1,0:T(8,128)(2,1)}), bf16[32,16,768]{2,1,0:T(8,128)(2,1)S(1)}, u32[]{:S(2)}, u32[]{:S(2)}) %all-to-all-start) | async-done | bytes 786464 | tf_op jit(solution)/shard_map/all_to_all | solution.py:360
  37.2 4.3 %collective-permute-start.1 = (bf16[208,2048]{1,0:T(8,128)(2,1)S(1)}, bf16[208,2048]{1,0:T(8,128)(2,1)S(1)}, u32[]{:S(2)}, u32[]{:S(2)}) collective-permute-start(bf16[208,2048]{1,0:T(8,128)(2,1)S(1)} %collect.1.refs_0_), channel_id=1, source_target_pairs={{0,32},{1,225},{2,34},{3,227},{4,36},{5,229},{6,38},{7,231},{8,40}... | collective-permute-start | bytes 2555912 | tf_op jit(solution)/shard_map/ppermute | solution.py:288
  41.5 8.6 %collective-permute-start.3 = (bf16[208,2048]{1,0:T(8,128)(2,1)S(1)}, bf16[208,2048]{1,0:T(8,128)(2,1)S(1)}, u32[]{:S(2)}, u32[]{:S(2)}) collective-permute-start(bf16[208,2048]{1,0:T(8,128)(2,1)S(1)} %collect.1.refs_0_), channel_id=1, source_target_pairs={{0,224},{1,33},{2,226},{3,35},{4,228},{5,37},{6,230},{7,39},{8,232... | collective-permute-start | bytes 2555912 | tf_op jit(solution)/shard_map/ppermute | solution.py:288
  52.0 12.0 %collective-permute-done.1.refs_1_ = bf16[208,2048]{1,0:T(8,128)(2,1)S(1)} collective-permute-done((bf16[208,2048]{1,0:T(8,128)(2,1)S(1)}, bf16[208,2048]{1,0:T(8,128)(2,1)S(1)}, u32[]{:S(2)}, u32[]{:S(2)}) %collective-permute-start.1) | collective-permute-done | bytes 852000 | tf_op jit(solution)/shard_map/ppermute | solution.py:288
  66.4 6.2 %collective-permute-start.4 = (bf16[208,2048]{1,0:T(8,128)(2,1)S(1)}, bf16[208,2048]{1,0:T(8,128)(2,1)S(1)}, u32[]{:S(2)}, u32[]{:S(2)}) collective-permute-start(bf16[208,2048]{1,0:T(8,128)(2,1)S(1)} %collective-permute-done.3.refs_3_), channel_id=1, source_target_pairs={{0,224},{1,33},{2,226},{3,35},{4,228},{5,37},{6,230},{7,39},{8,232... | collective-permute-start | bytes 2555912 | tf_op jit(solution)/shard_map/ppermute | solution.py:288
  74.6 9.1 %collective-permute-done.5.refs_4_.refs_7_ = bf16[320,2048]{1,0:T(8,128)(2,1)S(1)} collective-permute-done((bf16[320,2048]{1,0:T(8,128)(2,1)S(1)}, bf16[320,2048]{1,0:T(8,128)(2,1)S(1)}, u32[]{:S(2)}, u32[]{:S(2)}) %collective-permute-start.5) | collective-permute-done | bytes 1310752 | tf_op jit(solution)/shard_map/ppermute | solution.py:292
  83.7 4.5 %collective-permute-done.2.refs_2_ = bf16[208,2048]{1,0:T(8,128)(2,1)S(1)} collective-permute-done((bf16[208,2048]{1,0:T(8,128)(2,1)S(1)}, bf16[208,2048]{1,0:T(8,128)(2,1)S(1)}, u32[]{:S(2)}, u32[]{:S(2)}) %collective-permute-start.2) | collective-permute-done | bytes 852000 | tf_op jit(solution)/shard_map/ppermute | solution.py:288
  88.2 6.0 %collective-permute-start.7 = (bf16[208,2048]{1,0:T(8,128)(2,1)S(1)}, bf16[208,2048]{1,0:T(8,128)(2,1)S(1)}, u32[]{:S(2)}, u32[]{:S(2)}) collective-permute-start(bf16[208,2048]{1,0:T(8,128)(2,1)S(1)} %collective-permute-done.4.refs_4_), channel_id=1, source_target_pairs={{0,224},{1,33},{2,226},{3,35},{4,228},{5,37},{6,230},{7,39},{8,232... | collective-permute-start | bytes 2555912 | tf_op jit(solution)/shard_map/ppermute | solution.py:288
  96.1 15.3 %collective-permute-done.7.refs_1_ = bf16[208,2048]{1,0:T(8,128)(2,1)S(1)} collective-permute-done((bf16[208,2048]{1,0:T(8,128)(2,1)S(1)}, bf16[208,2048]{1,0:T(8,128)(2,1)S(1)}, u32[]{:S(2)}, u32[]{:S(2)}) %collective-permute-start.7) | collective-permute-done | bytes 852000 | tf_op jit(solution)/shard_map/ppermute | solution.py:288
  111.4 5.6 %collective-permute-start.10 = (bf16[112,2048]{1,0:T(8,128)(2,1)S(1)}, bf16[112,2048]{1,0:T(8,128)(2,1)S(1)}, u32[]{:S(2)}, u32[]{:S(2)}) collective-permute-start(bf16[112,2048]{1,0:T(8,128)(2,1)S(1)} %slice.25), channel_id=1, source_target_pairs={{0,224},{1,33},{2,226},{3,35},{4,228},{5,37},{6,230},{7,39},{8,232... | collective-permute-start | bytes 1376264 | tf_op jit(solution)/shard_map/ppermute | solution.py:288
  119.0 3.9 %experts_third.1 = (bf16[96,2176]{1,0:T(8,128)(2,1)S(1)}, bf16[96,2176]{1,0:T(8,128)(2,1)S(1)}, bf16[32,2048]{1,0:T(8,128)(2,1)S(1)}) custom-call(bf16[208,2048]{1,0:T(8,128)(2,1)S(1)} %collective-permute-done.6.refs_0_, bf16[208,2048]{1,0:T(8,128)(2,1)S(1)} %collective-permute-done.7.refs_1_, bf16[320,2048]{1,0:T(8,128)(2,1)S(1)} %bitcast.41, ...), custom_call_target="tpu_custom_call" | custom-call | flops 1509949440 | tf_op jit(solution)/shard_map/experts_third/pallas_call | solution.py:57
  123.0 5.0 %collective-permute-done.9.refs_0_ = bf16[96,2048]{1,0:T(8,128)(2,1)S(1)} collective-permute-done((bf16[96,2048]{1,0:T(8,128)(2,1)S(1)}, bf16[96,2048]{1,0:T(8,128)(2,1)S(1)}, u32[]{:S(2)}, u32[]{:S(2)}) %collective-permute-start.9) | collective-permute-done | bytes 393248 | tf_op jit(solution)/shard_map/ppermute | solution.py:288
  139.7 4.4 %collective-permute-start.16 = (bf16[48,2176]{1,0:T(8,128)(2,1)S(1)}, bf16[48,2176]{1,0:T(8,128)(2,1)S(1)}, u32[]{:S(2)}, u32[]{:S(2)}) collective-permute-start(bf16[48,2176]{1,0:T(8,128)(2,1)S(1)} %get-tuple-element.52), channel_id=1, source_target_pairs={{0,64},{1,193},{2,66},{3,195},{4,68},{5,197},{6,70},{7,199},{8,72}... | collective-permute-start | bytes 626696 | tf_op jit(solution)/shard_map/ppermute | solution.py:288
  144.0 7.4 %experts_near.1 = (bf16[96,2176]{1,0:T(8,128)(2,1)S(1)}, bf16[96,2176]{1,0:T(8,128)(2,1)S(1)}, bf16[96,2176]{1,0:T(8,128)(2,1)S(1)}, bf16[96,2176]{1,0:T(8,128)(...) custom-call(bf16[208,2048]{1,0:T(8,128)(2,1)S(1)} %collect.1.refs_0_, ...), custom_call_target="tpu_custom_call" | custom-call | flops 3774873600 | tf_op jit(solution)/shard_map/experts_near/pallas_call | solution.py:57
  151.7 4.3 %collective-permute-start.13 = (bf16[96,2176]{1,0:T(8,128)(2,1)S(1)}, bf16[96,2176]{1,0:T(8,128)(2,1)S(1)}, u32[]{:S(2)}, u32[]{:S(2)}) collective-permute-start(bf16[96,2176]{1,0:T(8,128)(2,1)S(1)} %add_convert_fusion.3), channel_id=1, source_target_pairs={{0,224},{1,33},{2,226},{3,35},{4,228},{5,37},{6,230},{7,39},{8,232... | collective-permute-start | bytes 1253384 | tf_op jit(solution)/shard_map/ppermute | solution.py:288
  158.1 5.6 %collective-permute-done.13 = bf16[96,2176]{1,0:T(8,128)(2,1)S(1)} collective-permute-done((bf16[96,2176]{1,0:T(8,128)(2,1)S(1)}, bf16[96,2176]{1,0:T(8,128)(2,1)S(1)}, u32[]{:S(2)}, u32[]{:S(2)}) %collective-permute-start.13) | collective-permute-done | bytes 417824 | tf_op jit(solution)/shard_map/ppermute | solution.py:288
  163.8 5.0 %collective-permute-start.14 = (bf16[96,2176]{1,0:T(8,128)(2,1)S(1)}, bf16[96,2176]{1,0:T(8,128)(2,1)S(1)}, u32[]{:S(2)}, u32[]{:S(2)}) collective-permute-start(bf16[96,2176]{1,0:T(8,128)(2,1)S(1)} %add_convert_fusion.2), channel_id=1, source_target_pairs={{0,224},{1,33},{2,226},{3,35},{4,228},{5,37},{6,230},{7,39},{8,232... | collective-permute-start | bytes 1253384 | tf_op jit(solution)/shard_map/ppermute | solution.py:288
  170.8 6.1 %collective-permute-done.14.refs_1_ = bf16[96,2176]{1,0:T(8,128)(2,1)S(1)} collective-permute-done((bf16[96,2176]{1,0:T(8,128)(2,1)S(1)}, bf16[96,2176]{1,0:T(8,128)(2,1)S(1)}, u32[]{:S(2)}, u32[]{:S(2)}) %collective-permute-start.14) | collective-permute-done | bytes 417824 | tf_op jit(solution)/shard_map/ppermute | solution.py:288
  181.3 8.6 %all-to-all-start.1 = ((bf16[32,8,896]{2,1,0:T(8,128)(2,1)}), bf16[32,8,896]{2,1,0:T(8,128)(2,1)S(1)}, u32[]{:S(2)}, u32[]{:S(2)}) async-start(bf16[32,8,896]{2,1,0:T(8,128)(2,1)} %bitcast.12), calls=%async_computation.1 | async-start | bytes 917504 | tf_op jit(solution)/shard_map/all_to_all | solution.py:410
  193.2 10.4 %all-to-all-done.1 = bf16[32,8,896]{2,1,0:T(8,128)(2,1)S(1)} async-done(((bf16[32,8,896]{2,1,0:T(8,128)(2,1)}), bf16[32,8,896]{2,1,0:T(8,128)(2,1)S(1)}, u32[]{:S(2)}, u32[]{:S(2)}) %all-to-all-start.1) | async-done | bytes 458784 | tf_op jit(solution)/shard_map/all_to_all | solution.py:410
  205.4 4.8 %stream.1 = (bf16[128,2048]{1,0:T(8,128)(2,1)}, bf16[2048,128]{1,0:T(8,128)(2,1)S(1)}) custom-call(bf16[256,896]{1,0:T(8,128)(2,1)S(1)} %bitcast.51, f32[40,128]{1,0:T(8,128)S(1)} %copy-done.10, f32[8,384,128]{2,1,0:T(8,128)S(1)} %probs.1.refs_2_, bf16[32,2048]{1,0:T(8,128)(2,1)S(1)} %bitcast.57, bf16[128,2048]{1,0:T(8,128)(2,1)S(1)} %bitcast.54, ...), custom_call_target="tpu_custom_call" | custom-call | flops 671088640 | tf_op jit(solution)/shard_map/stream/pallas_call | solution.py:57
  210.2 23.4 %all_to_all.31 = bf16[16,128,128]{2,1,0:T(8,128)(2,1)S(1)} all-to-all(bf16[16,128,128]{2,1,0:T(8,128)(2,1)S(1)} %bitcast.52), channel_id=1, replica_groups=mesh['seq'=16,'exp'=32] {'seq'}, dimensions={0} | all-to-all | bytes 1048576 | tf_op jit(solution)/shard_map/all_to_all | solution.py:423
  (65 shorter events, 42.5 us)
Async XLA Ops:
  3.9 46.2 %copy-start = (bf16[1,2048,320]{1,2,0:T(8,128)(2,1)S(1)}, bf16[1,2048,320]{1,2,0:T(8,128)(2,1)}, u32[]{:S(2)}) copy-start(bf16[1,2048,320]{1,2,0:T(8,128)(2,1)} %param.18) | copy-start | bytes 3932164
  3.9 68.8 %copy-start.1 = (bf16[1,320,2048]{2,1,0:T(8,128)(2,1)S(1)}, bf16[1,320,2048]{2,1,0:T(8,128)(2,1)}, u32[]{:S(2)}) copy-start(bf16[1,320,2048]{2,1,0:T(8,128)(2,1)} %param.19) | copy-start | bytes 3932164
  3.9 32.6 %all-to-all-start = ((bf16[32,16,768]{2,1,0:T(8,128)(2,1)}), bf16[32,16,768]{2,1,0:T(8,128)(2,1)S(1)}, u32[]{:S(2)}, u32[]{:S(2)}) async-start(bf16[32,16,768]{2,1,0:T(8,128)(2,1)} %bitcast.60), calls=%async_computation | async-start | bytes 1572864 | tf_op jit(solution)/shard_map/all_to_all | solution.py:360
  14.3 17.6 %collective-permute-start = (bf16[128,128]{1,0:T(8,128)(2,1)S(1)}, bf16[128,128]{1,0:T(8,128)(2,1)S(1)}, u32[]{:S(2)}, u32[]{:S(2)}) collective-permute-start(bf16[128,128]{1,0:T(8,128)(2,1)S(1)} %pad_maximum_fusion.kv_ref), channel_id=1, source_target_pairs={{0,256},{32,288},{64,320},{96,352},{128,384},{160,416},{192,448},{... | collective-permute-start | bytes 98312 | tf_op jit(solution)/shard_map/ppermute | solution.py:292
  37.2 26.9 %collective-permute-start.1 = (bf16[208,2048]{1,0:T(8,128)(2,1)S(1)}, bf16[208,2048]{1,0:T(8,128)(2,1)S(1)}, u32[]{:S(2)}, u32[]{:S(2)}) collective-permute-start(bf16[208,2048]{1,0:T(8,128)(2,1)S(1)} %collect.1.refs_0_), channel_id=1, source_target_pairs={{0,32},{1,225},{2,34},{3,227},{4,36},{5,229},{6,38},{7,231},{8,40}... | collective-permute-start | bytes 2555912 | tf_op jit(solution)/shard_map/ppermute | solution.py:288
  41.5 24.9 %collective-permute-start.3 = (bf16[208,2048]{1,0:T(8,128)(2,1)S(1)}, bf16[208,2048]{1,0:T(8,128)(2,1)S(1)}, u32[]{:S(2)}, u32[]{:S(2)}) collective-permute-start(bf16[208,2048]{1,0:T(8,128)(2,1)S(1)} %collect.1.refs_0_), channel_id=1, source_target_pairs={{0,224},{1,33},{2,226},{3,35},{4,228},{5,37},{6,230},{7,39},{8,232... | collective-permute-start | bytes 2555912 | tf_op jit(solution)/shard_map/ppermute | solution.py:288
  50.1 33.6 %collective-permute-start.5 = (bf16[320,2048]{1,0:T(8,128)(2,1)S(1)}, bf16[320,2048]{1,0:T(8,128)(2,1)S(1)}, u32[]{:S(2)}, u32[]{:S(2)}) collective-permute-start(bf16[320,2048]{1,0:T(8,128)(2,1)S(1)} %bitcast.40), channel_id=1, source_target_pairs={{0,256},{32,288},{64,320},{96,352},{128,384},{160,416},{192,448},{... | collective-permute-start | bytes 3932168 | tf_op jit(solution)/shard_map/ppermute | solution.py:292
  64.1 24.1 %collective-permute-start.2 = (bf16[208,2048]{1,0:T(8,128)(2,1)S(1)}, bf16[208,2048]{1,0:T(8,128)(2,1)S(1)}, u32[]{:S(2)}, u32[]{:S(2)}) collective-permute-start(bf16[208,2048]{1,0:T(8,128)(2,1)S(1)} %collective-permute-done.1.refs_1_), channel_id=1, source_target_pairs={{0,32},{1,225},{2,34},{3,227},{4,36},{5,229},{6,38},{7,231},{8,40}... | collective-permute-start | bytes 2555912 | tf_op jit(solution)/shard_map/ppermute | solution.py:288
  66.4 21.7 %collective-permute-start.4 = (bf16[208,2048]{1,0:T(8,128)(2,1)S(1)}, bf16[208,2048]{1,0:T(8,128)(2,1)S(1)}, u32[]{:S(2)}, u32[]{:S(2)}) collective-permute-start(bf16[208,2048]{1,0:T(8,128)(2,1)S(1)} %collective-permute-done.3.refs_3_), channel_id=1, source_target_pairs={{0,224},{1,33},{2,226},{3,35},{4,228},{5,37},{6,230},{7,39},{8,232... | collective-permute-start | bytes 2555912 | tf_op jit(solution)/shard_map/ppermute | solution.py:288
  72.7 46.3 %collective-permute-start.8 = (bf16[320,2048]{1,0:T(8,128)(2,1)S(1)}, bf16[320,2048]{1,0:T(8,128)(2,1)S(1)}, u32[]{:S(2)}, u32[]{:S(2)}) collective-permute-start(bf16[320,2048]{1,0:T(8,128)(2,1)S(1)} %bitcast.44), channel_id=1, source_target_pairs={{0,256},{32,288},{64,320},{96,352},{128,384},{160,416},{192,448},{... | collective-permute-start | bytes 3932168 | tf_op jit(solution)/shard_map/ppermute | solution.py:292
  88.2 23.2 %collective-permute-start.7 = (bf16[208,2048]{1,0:T(8,128)(2,1)S(1)}, bf16[208,2048]{1,0:T(8,128)(2,1)S(1)}, u32[]{:S(2)}, u32[]{:S(2)}) collective-permute-start(bf16[208,2048]{1,0:T(8,128)(2,1)S(1)} %collective-permute-done.4.refs_4_), channel_id=1, source_target_pairs={{0,224},{1,33},{2,226},{3,35},{4,228},{5,37},{6,230},{7,39},{8,232... | collective-permute-start | bytes 2555912 | tf_op jit(solution)/shard_map/ppermute | solution.py:288
  94.1 22.9 %collective-permute-start.6 = (bf16[208,2048]{1,0:T(8,128)(2,1)S(1)}, bf16[208,2048]{1,0:T(8,128)(2,1)S(1)}, u32[]{:S(2)}, u32[]{:S(2)}) collective-permute-start(bf16[208,2048]{1,0:T(8,128)(2,1)S(1)} %collective-permute-done.2.refs_2_), channel_id=1, source_target_pairs={{0,32},{1,225},{2,34},{3,227},{4,36},{5,229},{6,38},{7,231},{8,40}... | collective-permute-start | bytes 2555912 | tf_op jit(solution)/shard_map/ppermute | solution.py:288
  111.4 22.4 %collective-permute-start.10 = (bf16[112,2048]{1,0:T(8,128)(2,1)S(1)}, bf16[112,2048]{1,0:T(8,128)(2,1)S(1)}, u32[]{:S(2)}, u32[]{:S(2)}) collective-permute-start(bf16[112,2048]{1,0:T(8,128)(2,1)S(1)} %slice.25), channel_id=1, source_target_pairs={{0,224},{1,33},{2,226},{3,35},{4,228},{5,37},{6,230},{7,39},{8,232... | collective-permute-start | bytes 1376264 | tf_op jit(solution)/shard_map/ppermute | solution.py:288
  117.1 10.9 %collective-permute-start.9 = (bf16[96,2048]{1,0:T(8,128)(2,1)S(1)}, bf16[96,2048]{1,0:T(8,128)(2,1)S(1)}, u32[]{:S(2)}, u32[]{:S(2)}) collective-permute-start(bf16[96,2048]{1,0:T(8,128)(2,1)S(1)} %slice.24), channel_id=1, source_target_pairs={{0,32},{1,225},{2,34},{3,227},{4,36},{5,229},{6,38},{7,231},{8,40}... | collective-permute-start | bytes 1179656 | tf_op jit(solution)/shard_map/ppermute | solution.py:288
  128.0 23.5 %collective-permute-start.11 = (bf16[96,2176]{1,0:T(8,128)(2,1)S(1)}, bf16[96,2176]{1,0:T(8,128)(2,1)S(1)}, u32[]{:S(2)}, u32[]{:S(2)}) collective-permute-start(bf16[96,2176]{1,0:T(8,128)(2,1)S(1)} %get-tuple-element.47), channel_id=1, source_target_pairs={{0,224},{1,33},{2,226},{3,35},{4,228},{5,37},{6,230},{7,39},{8,232... | collective-permute-start | bytes 1253384 | tf_op jit(solution)/shard_map/ppermute | solution.py:288
  129.9 26.1 %collective-permute-start.15 = (bf16[96,2176]{1,0:T(8,128)(2,1)S(1)}, bf16[96,2176]{1,0:T(8,128)(2,1)S(1)}, u32[]{:S(2)}, u32[]{:S(2)}) collective-permute-start(bf16[96,2176]{1,0:T(8,128)(2,1)S(1)} %get-tuple-element.51), channel_id=1, source_target_pairs={{0,32},{1,225},{2,34},{3,227},{4,36},{5,229},{6,38},{7,231},{8,40}... | collective-permute-start | bytes 1253384 | tf_op jit(solution)/shard_map/ppermute | solution.py:288
  137.1 14.4 %copy-start.8 = (bf16[16,2048]{1,0:T(8,128)(2,1)}, bf16[16,2048]{1,0:T(8,128)(2,1)S(1)}, u32[]{:S(2)}) copy-start(bf16[16,2048]{1,0:T(8,128)(2,1)S(1)} %get-tuple-element.56.refs_2_) | copy-start | bytes 196612
  137.1 14.4 %collective-permute-start.12 = (bf16[48,2176]{1,0:T(8,128)(2,1)S(1)}, bf16[48,2176]{1,0:T(8,128)(2,1)S(1)}, u32[]{:S(2)}, u32[]{:S(2)}) collective-permute-start(bf16[48,2176]{1,0:T(8,128)(2,1)S(1)} %get-tuple-element.48), channel_id=1, source_target_pairs={{0,192},{1,65},{2,194},{3,67},{4,196},{5,69},{6,198},{7,71},{8,200... | collective-permute-start | bytes 626696 | tf_op jit(solution)/shard_map/ppermute | solution.py:288
  139.7 16.3 %collective-permute-start.16 = (bf16[48,2176]{1,0:T(8,128)(2,1)S(1)}, bf16[48,2176]{1,0:T(8,128)(2,1)S(1)}, u32[]{:S(2)}, u32[]{:S(2)}) collective-permute-start(bf16[48,2176]{1,0:T(8,128)(2,1)S(1)} %get-tuple-element.52), channel_id=1, source_target_pairs={{0,64},{1,193},{2,66},{3,195},{4,68},{5,197},{6,70},{7,199},{8,72}... | collective-permute-start | bytes 626696 | tf_op jit(solution)/shard_map/ppermute | solution.py:288
  151.7 12.0 %collective-permute-start.13 = (bf16[96,2176]{1,0:T(8,128)(2,1)S(1)}, bf16[96,2176]{1,0:T(8,128)(2,1)S(1)}, u32[]{:S(2)}, u32[]{:S(2)}) collective-permute-start(bf16[96,2176]{1,0:T(8,128)(2,1)S(1)} %add_convert_fusion.3), channel_id=1, source_target_pairs={{0,224},{1,33},{2,226},{3,35},{4,228},{5,37},{6,230},{7,39},{8,232... | collective-permute-start | bytes 1253384 | tf_op jit(solution)/shard_map/ppermute | solution.py:288
  156.2 12.6 %collective-permute-start.17 = (bf16[96,2176]{1,0:T(8,128)(2,1)S(1)}, bf16[96,2176]{1,0:T(8,128)(2,1)S(1)}, u32[]{:S(2)}, u32[]{:S(2)}) collective-permute-start(bf16[96,2176]{1,0:T(8,128)(2,1)S(1)} %add_convert_fusion.1), channel_id=1, source_target_pairs={{0,32},{1,225},{2,34},{3,227},{4,36},{5,229},{6,38},{7,231},{8,40}... | collective-permute-start | bytes 1253384 | tf_op jit(solution)/shard_map/ppermute | solution.py:288
  163.8 13.2 %collective-permute-start.14 = (bf16[96,2176]{1,0:T(8,128)(2,1)S(1)}, bf16[96,2176]{1,0:T(8,128)(2,1)S(1)}, u32[]{:S(2)}, u32[]{:S(2)}) collective-permute-start(bf16[96,2176]{1,0:T(8,128)(2,1)S(1)} %add_convert_fusion.2), channel_id=1, source_target_pairs={{0,224},{1,33},{2,226},{3,35},{4,228},{5,37},{6,230},{7,39},{8,232... | collective-permute-start | bytes 1253384 | tf_op jit(solution)/shard_map/ppermute | solution.py:288
  168.9 11.1 %collective-permute-start.18 = (bf16[96,2176]{1,0:T(8,128)(2,1)S(1)}, bf16[96,2176]{1,0:T(8,128)(2,1)S(1)}, u32[]{:S(2)}, u32[]{:S(2)}) collective-permute-start(bf16[96,2176]{1,0:T(8,128)(2,1)S(1)} %add_convert_fusion), channel_id=1, source_target_pairs={{0,32},{1,225},{2,34},{3,227},{4,36},{5,229},{6,38},{7,231},{8,40}... | collective-permute-start | bytes 1253384 | tf_op jit(solution)/shard_map/ppermute | solution.py:288
  181.3 22.4 %all-to-all-start.1 = ((bf16[32,8,896]{2,1,0:T(8,128)(2,1)}), bf16[32,8,896]{2,1,0:T(8,128)(2,1)S(1)}, u32[]{:S(2)}, u32[]{:S(2)}) async-start(bf16[32,8,896]{2,1,0:T(8,128)(2,1)} %bitcast.12), calls=%async_computation.1 | async-start | bytes 917504 | tf_op jit(solution)/shard_map/all_to_all | solution.py:410
  (11 other events, 90.3 us)

commit v4 on v3

--- a/solution.py
+++ b/solution.py
@@ -82,7 +82,10 @@
 ):
     stream = resid_ref()[...].astype(F32)
     root_mean = jnp.sqrt(jnp.mean(stream * stream, axis=-1, keepdims=True) + EPSILON)
-    normed_in = (stream / root_mean * gain_ref()[...]).astype(BF16)
+    gain = gain_ref()[...]
+    normed_in = (stream / root_mean * gain).astype(BF16)
+    for i in range(16):
+        token_ref[EXPERTS + 8 + i : EXPERTS + 9 + i] = gain[:, i * 128 : (i + 1) * 128]
     ids, slot = ids_ref()[...], slot_ref()[...]
     target = jnp.where(slot < CAP, slot * EXPERTS + ids, -1).astype(F32)
     logits = logits_ref()[...]
@@ -185,7 +188,7 @@
 
 
 def stream_kernel(
-    in_ref, token_ref, probs_ref, weight_ref, resid_ref, gain_ref, grad_ref, query_ref,
+    in_ref, token_ref, probs_ref, weight_ref, resid_ref, grad_ref, query_ref,
     out_ref, terms_ref, rows_ref,
 ):
     rows = dot(shuffle_matrix(8), in_ref[...], ((0,), (0,))).astype(BF16)
@@ -208,7 +211,10 @@
     stream = resid_ref()[...].astype(F32)
     root_mean = jnp.sqrt(jnp.mean(stream * stream, axis=-1, keepdims=True) + EPSILON)
     normed = stream / root_mean
-    normed_grad = (chosen * fetched + router_term) * gain_ref()[...]
+    gain = jnp.concatenate(
+        [token_ref[EXPERTS + 8 + i : EXPERTS + 9 + i] for i in range(16)], axis=1
+    )
+    normed_grad = (chosen * fetched + router_term) * gain
     mean = jnp.mean(normed_grad * normed, axis=-1, keepdims=True)
     out_ref[...] = (
         grad_ref()[...].astype(F32) + (normed_grad - normed * mean) / root_mean
@@ -350,7 +356,7 @@
     outgoing, token_rows = call(
         dispatch_kernel,
         [stream, upstream, gain, expert_index, slot, router_logits[0].T],
-        [shape((512, 768)), shape((EXPERTS + 8, TOK), F32)],
+        [shape((512, 768)), shape((EXPERTS + 24, TOK), F32)],
         hbm=(0, 1, 2, 3, 4, 5),
         scratch=[pltpu.VMEM((512, 768), BF16)],
         flops=2 * 512 * 512 * 768,
@@ -411,10 +417,10 @@
     grad_stream, terms = call(
         stream_kernel,
         [
-            returned, token_rows, probs, router_weight.T, stream, gain, upstream, query,
+            returned, token_rows, probs, router_weight.T, stream, upstream, query,
         ],
         [shape((TOK, D)), shape((2048, 128))],
-        hbm=(1, 2, 3, 4, 5, 6, 7),
+        hbm=(1, 2, 3, 4, 5, 6),
         scratch=[pltpu.VMEM((SLOTS, WIDE), BF16)],
         flops=2 * 512 * 512 * 512 + 8 * 3 * 2 * 256 * 256 * 128,
         limit=20,

time: 237 us -> 237 us (level)
  no operation moved by 1% of the time
where the time goes in v4:
time: 237 us; the launch traced here: 234 us
  waiting for transfers between devices  91.1 us (38%)
  starting transfers between devices  87.7 us (37%)
  Pallas kernels  25.7 us (11%)
  blocking collectives  23.4 us (10%)
  local copies, waits for them, and re-layouts  4.33 us (2%)
    ppermute x16, starting transfers between devices, shift(): return lax.ppermute(a, ('seq', 'exp'), pairs)  62.4 us
    ppermute x16, waiting for transfers between devices, shift(): return lax.ppermute(a, ('seq', 'exp'), pairs)  52 us
    pallas_call x7, Pallas kernels, call(): pl.pallas_call(run if hbm else kernel, in_specs=specs, out_specs=[pl.Bloc...  24.4 us
    ppermute x3, waiting for transfers between devices, across(): lax.ppermute(a, 'seq', [(s, (s + N_Z) % (N_Y * N_Z)) for s in range(N_Y *...  24.1 us
    all_to_all x1, blocking collectives, body(): terms = lax.all_to_all(terms, 'seq', 0, 0, tiled=True)  23.4 us
    all_to_all x1, waiting for transfers between devices, body(): returned = lax.all_to_all(returning, 'exp', 0, 0, tiled=True)  10.4 us
    all_to_all x1, starting transfers between devices, body(): arrived = lax.all_to_all(outgoing, 'exp', 0, 0, tiled=True)  10.4 us
    all_to_all x1, starting transfers between devices, body(): returned = lax.all_to_all(returning, 'exp', 0, 0, tiled=True)  8.54 us
  transfers between devices with their start and end apart: 21, of which 12 were waited for; matrix products, arithmetic and copies ran while one was open for 0% of the time, Pallas kernels for 7%

profile of v4, /device:TPU:6, one launch (start us, length us, event | category | flops | bytes accessed | tf_op | source)
XLA Modules:
  0.0 234.2 jit_solution(1322637341565535305)
XLA Ops:
  3.9 10.4 %all-to-all-start = ((bf16[32,16,768]{2,1,0:T(8,128)(2,1)}), bf16[32,16,768]{2,1,0:T(8,128)(2,1)S(1)}, u32[]{:S(2)}, u32[]{:S(2)}) async-start(bf16[32,16,768]{2,1,0:T(8,128)(2,1)} %bitcast.58), calls=%async_computation | async-start | bytes 1572864 | tf_op jit(solution)/shard_map/all_to_all | solution.py:366
  17.0 15.0 %collective-permute-done.kv_other_ref = bf16[128,128]{1,0:T(8,128)(2,1)S(1)} collective-permute-done((bf16[128,128]{1,0:T(8,128)(2,1)S(1)}, bf16[128,128]{1,0:T(8,128)(2,1)S(1)}, u32[]{:S(2)}, u32[]{:S(2)}) %collective-permute-start) | collective-permute-done | bytes 32800 | tf_op jit(solution)/shard_map/ppermute | solution.py:298
  32.0 4.6 %all-to-all-done = bf16[32,16,768]{2,1,0:T(8,128)(2,1)S(1)} async-done(((bf16[32,16,768]{2,1,0:T(8,128)(2,1)}), bf16[32,16,768]{2,1,0:T(8,128)(2,1)S(1)}, u32[]{:S(2)}, u32[]{:S(2)}) %all-to-all-start) | async-done | bytes 786464 | tf_op jit(solution)/shard_map/all_to_all | solution.py:366
  37.2 4.3 %collective-permute-start.1 = (bf16[208,2048]{1,0:T(8,128)(2,1)S(1)}, bf16[208,2048]{1,0:T(8,128)(2,1)S(1)}, u32[]{:S(2)}, u32[]{:S(2)}) collective-permute-start(bf16[208,2048]{1,0:T(8,128)(2,1)S(1)} %collect.1.refs_0_), channel_id=1, source_target_pairs={{0,32},{1,225},{2,34},{3,227},{4,36},{5,229},{6,38},{7,231},{8,40}... | collective-permute-start | bytes 2555912 | tf_op jit(solution)/shard_map/ppermute | solution.py:294
  41.5 8.6 %collective-permute-start.3 = (bf16[208,2048]{1,0:T(8,128)(2,1)S(1)}, bf16[208,2048]{1,0:T(8,128)(2,1)S(1)}, u32[]{:S(2)}, u32[]{:S(2)}) collective-permute-start(bf16[208,2048]{1,0:T(8,128)(2,1)S(1)} %collect.1.refs_0_), channel_id=1, source_target_pairs={{0,224},{1,33},{2,226},{3,35},{4,228},{5,37},{6,230},{7,39},{8,232... | collective-permute-start | bytes 2555912 | tf_op jit(solution)/shard_map/ppermute | solution.py:294
  52.0 12.0 %collective-permute-done.1.refs_1_ = bf16[208,2048]{1,0:T(8,128)(2,1)S(1)} collective-permute-done((bf16[208,2048]{1,0:T(8,128)(2,1)S(1)}, bf16[208,2048]{1,0:T(8,128)(2,1)S(1)}, u32[]{:S(2)}, u32[]{:S(2)}) %collective-permute-start.1) | collective-permute-done | bytes 852000 | tf_op jit(solution)/shard_map/ppermute | solution.py:294
  66.4 6.2 %collective-permute-start.4 = (bf16[208,2048]{1,0:T(8,128)(2,1)S(1)}, bf16[208,2048]{1,0:T(8,128)(2,1)S(1)}, u32[]{:S(2)}, u32[]{:S(2)}) collective-permute-start(bf16[208,2048]{1,0:T(8,128)(2,1)S(1)} %collective-permute-done.3.refs_3_), channel_id=1, source_target_pairs={{0,224},{1,33},{2,226},{3,35},{4,228},{5,37},{6,230},{7,39},{8,232... | collective-permute-start | bytes 2555912 | tf_op jit(solution)/shard_map/ppermute | solution.py:294
  74.6 9.1 %collective-permute-done.5.refs_4_.refs_7_ = bf16[320,2048]{1,0:T(8,128)(2,1)S(1)} collective-permute-done((bf16[320,2048]{1,0:T(8,128)(2,1)S(1)}, bf16[320,2048]{1,0:T(8,128)(2,1)S(1)}, u32[]{:S(2)}, u32[]{:S(2)}) %collective-permute-start.5) | collective-permute-done | bytes 1310752 | tf_op jit(solution)/shard_map/ppermute | solution.py:298
  83.7 4.4 %collective-permute-done.2.refs_2_ = bf16[208,2048]{1,0:T(8,128)(2,1)S(1)} collective-permute-done((bf16[208,2048]{1,0:T(8,128)(2,1)S(1)}, bf16[208,2048]{1,0:T(8,128)(2,1)S(1)}, u32[]{:S(2)}, u32[]{:S(2)}) %collective-permute-start.2) | collective-permute-done | bytes 852000 | tf_op jit(solution)/shard_map/ppermute | solution.py:294
  88.1 6.0 %collective-permute-start.7 = (bf16[208,2048]{1,0:T(8,128)(2,1)S(1)}, bf16[208,2048]{1,0:T(8,128)(2,1)S(1)}, u32[]{:S(2)}, u32[]{:S(2)}) collective-permute-start(bf16[208,2048]{1,0:T(8,128)(2,1)S(1)} %collective-permute-done.4.refs_4_), channel_id=1, source_target_pairs={{0,224},{1,33},{2,226},{3,35},{4,228},{5,37},{6,230},{7,39},{8,232... | collective-permute-start | bytes 2555912 | tf_op jit(solution)/shard_map/ppermute | solution.py:294
  96.0 15.3 %collective-permute-done.7.refs_1_ = bf16[208,2048]{1,0:T(8,128)(2,1)S(1)} collective-permute-done((bf16[208,2048]{1,0:T(8,128)(2,1)S(1)}, bf16[208,2048]{1,0:T(8,128)(2,1)S(1)}, u32[]{:S(2)}, u32[]{:S(2)}) %collective-permute-start.7) | collective-permute-done | bytes 852000 | tf_op jit(solution)/shard_map/ppermute | solution.py:294
  111.4 5.6 %collective-permute-start.10 = (bf16[112,2048]{1,0:T(8,128)(2,1)S(1)}, bf16[112,2048]{1,0:T(8,128)(2,1)S(1)}, u32[]{:S(2)}, u32[]{:S(2)}) collective-permute-start(bf16[112,2048]{1,0:T(8,128)(2,1)S(1)} %slice.25), channel_id=1, source_target_pairs={{0,224},{1,33},{2,226},{3,35},{4,228},{5,37},{6,230},{7,39},{8,232... | collective-permute-start | bytes 1376264 | tf_op jit(solution)/shard_map/ppermute | solution.py:294
  119.0 3.9 %experts_third.1 = (bf16[96,2176]{1,0:T(8,128)(2,1)S(1)}, bf16[96,2176]{1,0:T(8,128)(2,1)S(1)}, bf16[32,2048]{1,0:T(8,128)(2,1)S(1)}) custom-call(bf16[208,2048]{1,0:T(8,128)(2,1)S(1)} %collective-permute-done.6.refs_0_, bf16[208,2048]{1,0:T(8,128)(2,1)S(1)} %collective-permute-done.7.refs_1_, bf16[320,2048]{1,0:T(8,128)(2,1)S(1)} %bitcast.41, ...), custom_call_target="tpu_custom_call" | custom-call | flops 1509949440 | tf_op jit(solution)/shard_map/experts_third/pallas_call | solution.py:57
  122.9 5.0 %collective-permute-done.9.refs_0_ = bf16[96,2048]{1,0:T(8,128)(2,1)S(1)} collective-permute-done((bf16[96,2048]{1,0:T(8,128)(2,1)S(1)}, bf16[96,2048]{1,0:T(8,128)(2,1)S(1)}, u32[]{:S(2)}, u32[]{:S(2)}) %collective-permute-start.9) | collective-permute-done | bytes 393248 | tf_op jit(solution)/shard_map/ppermute | solution.py:294
  139.7 4.3 %collective-permute-start.16 = (bf16[48,2176]{1,0:T(8,128)(2,1)S(1)}, bf16[48,2176]{1,0:T(8,128)(2,1)S(1)}, u32[]{:S(2)}, u32[]{:S(2)}) collective-permute-start(bf16[48,2176]{1,0:T(8,128)(2,1)S(1)} %get-tuple-element.52), channel_id=1, source_target_pairs={{0,64},{1,193},{2,66},{3,195},{4,68},{5,197},{6,70},{7,199},{8,72}... | collective-permute-start | bytes 626696 | tf_op jit(solution)/shard_map/ppermute | solution.py:294
  144.0 7.4 %experts_near.1 = (bf16[96,2176]{1,0:T(8,128)(2,1)S(1)}, bf16[96,2176]{1,0:T(8,128)(2,1)S(1)}, bf16[96,2176]{1,0:T(8,128)(2,1)S(1)}, bf16[96,2176]{1,0:T(8,128)(...) custom-call(bf16[208,2048]{1,0:T(8,128)(2,1)S(1)} %collect.1.refs_0_, ...), custom_call_target="tpu_custom_call" | custom-call | flops 3774873600 | tf_op jit(solution)/shard_map/experts_near/pallas_call | solution.py:57
  151.6 4.3 %collective-permute-start.13 = (bf16[96,2176]{1,0:T(8,128)(2,1)S(1)}, bf16[96,2176]{1,0:T(8,128)(2,1)S(1)}, u32[]{:S(2)}, u32[]{:S(2)}) collective-permute-start(bf16[96,2176]{1,0:T(8,128)(2,1)S(1)} %add_convert_fusion.3), channel_id=1, source_target_pairs={{0,224},{1,33},{2,226},{3,35},{4,228},{5,37},{6,230},{7,39},{8,232... | collective-permute-start | bytes 1253384 | tf_op jit(solution)/shard_map/ppermute | solution.py:294
  158.0 5.6 %collective-permute-done.13 = bf16[96,2176]{1,0:T(8,128)(2,1)S(1)} collective-permute-done((bf16[96,2176]{1,0:T(8,128)(2,1)S(1)}, bf16[96,2176]{1,0:T(8,128)(2,1)S(1)}, u32[]{:S(2)}, u32[]{:S(2)}) %collective-permute-start.13) | collective-permute-done | bytes 417824 | tf_op jit(solution)/shard_map/ppermute | solution.py:294
  163.7 5.0 %collective-permute-start.14 = (bf16[96,2176]{1,0:T(8,128)(2,1)S(1)}, bf16[96,2176]{1,0:T(8,128)(2,1)S(1)}, u32[]{:S(2)}, u32[]{:S(2)}) collective-permute-start(bf16[96,2176]{1,0:T(8,128)(2,1)S(1)} %add_convert_fusion.2), channel_id=1, source_target_pairs={{0,224},{1,33},{2,226},{3,35},{4,228},{5,37},{6,230},{7,39},{8,232... | collective-permute-start | bytes 1253384 | tf_op jit(solution)/shard_map/ppermute | solution.py:294
  170.8 6.2 %collective-permute-done.14.refs_1_ = bf16[96,2176]{1,0:T(8,128)(2,1)S(1)} collective-permute-done((bf16[96,2176]{1,0:T(8,128)(2,1)S(1)}, bf16[96,2176]{1,0:T(8,128)(2,1)S(1)}, u32[]{:S(2)}, u32[]{:S(2)}) %collective-permute-start.14) | collective-permute-done | bytes 417824 | tf_op jit(solution)/shard_map/ppermute | solution.py:294
  181.2 8.5 %all-to-all-start.1 = ((bf16[32,8,896]{2,1,0:T(8,128)(2,1)}), bf16[32,8,896]{2,1,0:T(8,128)(2,1)S(1)}, u32[]{:S(2)}, u32[]{:S(2)}) async-start(bf16[32,8,896]{2,1,0:T(8,128)(2,1)} %bitcast.12), calls=%async_computation.1 | async-start | bytes 917504 | tf_op jit(solution)/shard_map/all_to_all | solution.py:416
  193.1 10.4 %all-to-all-done.1 = bf16[32,8,896]{2,1,0:T(8,128)(2,1)S(1)} async-done(((bf16[32,8,896]{2,1,0:T(8,128)(2,1)}), bf16[32,8,896]{2,1,0:T(8,128)(2,1)S(1)}, u32[]{:S(2)}, u32[]{:S(2)}) %all-to-all-start.1) | async-done | bytes 458784 | tf_op jit(solution)/shard_map/all_to_all | solution.py:416
  205.3 4.7 %stream.1 = (bf16[128,2048]{1,0:T(8,128)(2,1)}, bf16[2048,128]{1,0:T(8,128)(2,1)S(1)}) custom-call(bf16[256,896]{1,0:T(8,128)(2,1)S(1)} %bitcast.51, f32[56,128]{1,0:T(8,128)S(1)} %copy-done.10, f32[8,384,128]{2,1,0:T(8,128)S(1)} %probs.1.refs_2_, bf16[32,2048]{1,0:T(8,128)(2,1)S(1)} %bitcast.57, bf16[128,2048]{1,0:T(8,128)(2,1)S(1)} %bitcast.54, ...), custom_call_target="tpu_custom_call" | custom-call | flops 671088640 | tf_op jit(solution)/shard_map/stream/pallas_call | solution.py:57
  210.0 23.4 %all_to_all.31 = bf16[16,128,128]{2,1,0:T(8,128)(2,1)S(1)} all-to-all(bf16[16,128,128]{2,1,0:T(8,128)(2,1)S(1)} %bitcast.52), channel_id=1, replica_groups=mesh['seq'=16,'exp'=32] {'seq'}, dimensions={0} | all-to-all | bytes 1048576 | tf_op jit(solution)/shard_map/all_to_all | solution.py:429
  (63 shorter events, 42.6 us)
Async XLA Ops:
  3.9 46.2 %copy-start = (bf16[1,2048,320]{1,2,0:T(8,128)(2,1)S(1)}, bf16[1,2048,320]{1,2,0:T(8,128)(2,1)}, u32[]{:S(2)}) copy-start(bf16[1,2048,320]{1,2,0:T(8,128)(2,1)} %param.18) | copy-start | bytes 3932164
  3.9 68.7 %copy-start.1 = (bf16[1,320,2048]{2,1,0:T(8,128)(2,1)S(1)}, bf16[1,320,2048]{2,1,0:T(8,128)(2,1)}, u32[]{:S(2)}) copy-start(bf16[1,320,2048]{2,1,0:T(8,128)(2,1)} %param.19) | copy-start | bytes 3932164
  3.9 32.6 %all-to-all-start = ((bf16[32,16,768]{2,1,0:T(8,128)(2,1)}), bf16[32,16,768]{2,1,0:T(8,128)(2,1)S(1)}, u32[]{:S(2)}, u32[]{:S(2)}) async-start(bf16[32,16,768]{2,1,0:T(8,128)(2,1)} %bitcast.58), calls=%async_computation | async-start | bytes 1572864 | tf_op jit(solution)/shard_map/all_to_all | solution.py:366
  14.4 17.6 %collective-permute-start = (bf16[128,128]{1,0:T(8,128)(2,1)S(1)}, bf16[128,128]{1,0:T(8,128)(2,1)S(1)}, u32[]{:S(2)}, u32[]{:S(2)}) collective-permute-start(bf16[128,128]{1,0:T(8,128)(2,1)S(1)} %pad_maximum_fusion.kv_ref), channel_id=1, source_target_pairs={{0,256},{32,288},{64,320},{96,352},{128,384},{160,416},{192,448},{... | collective-permute-start | bytes 98312 | tf_op jit(solution)/shard_map/ppermute | solution.py:298
  37.2 26.9 %collective-permute-start.1 = (bf16[208,2048]{1,0:T(8,128)(2,1)S(1)}, bf16[208,2048]{1,0:T(8,128)(2,1)S(1)}, u32[]{:S(2)}, u32[]{:S(2)}) collective-permute-start(bf16[208,2048]{1,0:T(8,128)(2,1)S(1)} %collect.1.refs_0_), channel_id=1, source_target_pairs={{0,32},{1,225},{2,34},{3,227},{4,36},{5,229},{6,38},{7,231},{8,40}... | collective-permute-start | bytes 2555912 | tf_op jit(solution)/shard_map/ppermute | solution.py:294
  41.5 24.9 %collective-permute-start.3 = (bf16[208,2048]{1,0:T(8,128)(2,1)S(1)}, bf16[208,2048]{1,0:T(8,128)(2,1)S(1)}, u32[]{:S(2)}, u32[]{:S(2)}) collective-permute-start(bf16[208,2048]{1,0:T(8,128)(2,1)S(1)} %collect.1.refs_0_), channel_id=1, source_target_pairs={{0,224},{1,33},{2,226},{3,35},{4,228},{5,37},{6,230},{7,39},{8,232... | collective-permute-start | bytes 2555912 | tf_op jit(solution)/shard_map/ppermute | solution.py:294
  50.1 33.6 %collective-permute-start.5 = (bf16[320,2048]{1,0:T(8,128)(2,1)S(1)}, bf16[320,2048]{1,0:T(8,128)(2,1)S(1)}, u32[]{:S(2)}, u32[]{:S(2)}) collective-permute-start(bf16[320,2048]{1,0:T(8,128)(2,1)S(1)} %bitcast.40), channel_id=1, source_target_pairs={{0,256},{32,288},{64,320},{96,352},{128,384},{160,416},{192,448},{... | collective-permute-start | bytes 3932168 | tf_op jit(solution)/shard_map/ppermute | solution.py:298
  64.1 24.0 %collective-permute-start.2 = (bf16[208,2048]{1,0:T(8,128)(2,1)S(1)}, bf16[208,2048]{1,0:T(8,128)(2,1)S(1)}, u32[]{:S(2)}, u32[]{:S(2)}) collective-permute-start(bf16[208,2048]{1,0:T(8,128)(2,1)S(1)} %collective-permute-done.1.refs_1_), channel_id=1, source_target_pairs={{0,32},{1,225},{2,34},{3,227},{4,36},{5,229},{6,38},{7,231},{8,40}... | collective-permute-start | bytes 2555912 | tf_op jit(solution)/shard_map/ppermute | solution.py:294
  66.4 21.7 %collective-permute-start.4 = (bf16[208,2048]{1,0:T(8,128)(2,1)S(1)}, bf16[208,2048]{1,0:T(8,128)(2,1)S(1)}, u32[]{:S(2)}, u32[]{:S(2)}) collective-permute-start(bf16[208,2048]{1,0:T(8,128)(2,1)S(1)} %collective-permute-done.3.refs_3_), channel_id=1, source_target_pairs={{0,224},{1,33},{2,226},{3,35},{4,228},{5,37},{6,230},{7,39},{8,232... | collective-permute-start | bytes 2555912 | tf_op jit(solution)/shard_map/ppermute | solution.py:294
  72.7 46.3 %collective-permute-start.8 = (bf16[320,2048]{1,0:T(8,128)(2,1)S(1)}, bf16[320,2048]{1,0:T(8,128)(2,1)S(1)}, u32[]{:S(2)}, u32[]{:S(2)}) collective-permute-start(bf16[320,2048]{1,0:T(8,128)(2,1)S(1)} %bitcast.44), channel_id=1, source_target_pairs={{0,256},{32,288},{64,320},{96,352},{128,384},{160,416},{192,448},{... | collective-permute-start | bytes 3932168 | tf_op jit(solution)/shard_map/ppermute | solution.py:298
  88.1 23.2 %collective-permute-start.7 = (bf16[208,2048]{1,0:T(8,128)(2,1)S(1)}, bf16[208,2048]{1,0:T(8,128)(2,1)S(1)}, u32[]{:S(2)}, u32[]{:S(2)}) collective-permute-start(bf16[208,2048]{1,0:T(8,128)(2,1)S(1)} %collective-permute-done.4.refs_4_), channel_id=1, source_target_pairs={{0,224},{1,33},{2,226},{3,35},{4,228},{5,37},{6,230},{7,39},{8,232... | collective-permute-start | bytes 2555912 | tf_op jit(solution)/shard_map/ppermute | solution.py:294
  94.1 22.9 %collective-permute-start.6 = (bf16[208,2048]{1,0:T(8,128)(2,1)S(1)}, bf16[208,2048]{1,0:T(8,128)(2,1)S(1)}, u32[]{:S(2)}, u32[]{:S(2)}) collective-permute-start(bf16[208,2048]{1,0:T(8,128)(2,1)S(1)} %collective-permute-done.2.refs_2_), channel_id=1, source_target_pairs={{0,32},{1,225},{2,34},{3,227},{4,36},{5,229},{6,38},{7,231},{8,40}... | collective-permute-start | bytes 2555912 | tf_op jit(solution)/shard_map/ppermute | solution.py:294
  111.4 22.4 %collective-permute-start.10 = (bf16[112,2048]{1,0:T(8,128)(2,1)S(1)}, bf16[112,2048]{1,0:T(8,128)(2,1)S(1)}, u32[]{:S(2)}, u32[]{:S(2)}) collective-permute-start(bf16[112,2048]{1,0:T(8,128)(2,1)S(1)} %slice.25), channel_id=1, source_target_pairs={{0,224},{1,33},{2,226},{3,35},{4,228},{5,37},{6,230},{7,39},{8,232... | collective-permute-start | bytes 1376264 | tf_op jit(solution)/shard_map/ppermute | solution.py:294
  117.0 10.9 %collective-permute-start.9 = (bf16[96,2048]{1,0:T(8,128)(2,1)S(1)}, bf16[96,2048]{1,0:T(8,128)(2,1)S(1)}, u32[]{:S(2)}, u32[]{:S(2)}) collective-permute-start(bf16[96,2048]{1,0:T(8,128)(2,1)S(1)} %slice.24), channel_id=1, source_target_pairs={{0,32},{1,225},{2,34},{3,227},{4,36},{5,229},{6,38},{7,231},{8,40}... | collective-permute-start | bytes 1179656 | tf_op jit(solution)/shard_map/ppermute | solution.py:294
  127.9 23.6 %collective-permute-start.11 = (bf16[96,2176]{1,0:T(8,128)(2,1)S(1)}, bf16[96,2176]{1,0:T(8,128)(2,1)S(1)}, u32[]{:S(2)}, u32[]{:S(2)}) collective-permute-start(bf16[96,2176]{1,0:T(8,128)(2,1)S(1)} %get-tuple-element.47), channel_id=1, source_target_pairs={{0,224},{1,33},{2,226},{3,35},{4,228},{5,37},{6,230},{7,39},{8,232... | collective-permute-start | bytes 1253384 | tf_op jit(solution)/shard_map/ppermute | solution.py:294
  129.8 26.1 %collective-permute-start.15 = (bf16[96,2176]{1,0:T(8,128)(2,1)S(1)}, bf16[96,2176]{1,0:T(8,128)(2,1)S(1)}, u32[]{:S(2)}, u32[]{:S(2)}) collective-permute-start(bf16[96,2176]{1,0:T(8,128)(2,1)S(1)} %get-tuple-element.51), channel_id=1, source_target_pairs={{0,32},{1,225},{2,34},{3,227},{4,36},{5,229},{6,38},{7,231},{8,40}... | collective-permute-start | bytes 1253384 | tf_op jit(solution)/shard_map/ppermute | solution.py:294
  137.0 14.4 %copy-start.8 = (bf16[16,2048]{1,0:T(8,128)(2,1)}, bf16[16,2048]{1,0:T(8,128)(2,1)S(1)}, u32[]{:S(2)}) copy-start(bf16[16,2048]{1,0:T(8,128)(2,1)S(1)} %get-tuple-element.56.refs_2_) | copy-start | bytes 196612
  137.1 14.4 %collective-permute-start.12 = (bf16[48,2176]{1,0:T(8,128)(2,1)S(1)}, bf16[48,2176]{1,0:T(8,128)(2,1)S(1)}, u32[]{:S(2)}, u32[]{:S(2)}) collective-permute-start(bf16[48,2176]{1,0:T(8,128)(2,1)S(1)} %get-tuple-element.48), channel_id=1, source_target_pairs={{0,192},{1,65},{2,194},{3,67},{4,196},{5,69},{6,198},{7,71},{8,200... | collective-permute-start | bytes 626696 | tf_op jit(solution)/shard_map/ppermute | solution.py:294
  139.7 16.3 %collective-permute-start.16 = (bf16[48,2176]{1,0:T(8,128)(2,1)S(1)}, bf16[48,2176]{1,0:T(8,128)(2,1)S(1)}, u32[]{:S(2)}, u32[]{:S(2)}) collective-permute-start(bf16[48,2176]{1,0:T(8,128)(2,1)S(1)} %get-tuple-element.52), channel_id=1, source_target_pairs={{0,64},{1,193},{2,66},{3,195},{4,68},{5,197},{6,70},{7,199},{8,72}... | collective-permute-start | bytes 626696 | tf_op jit(solution)/shard_map/ppermute | solution.py:294
  151.6 12.0 %collective-permute-start.13 = (bf16[96,2176]{1,0:T(8,128)(2,1)S(1)}, bf16[96,2176]{1,0:T(8,128)(2,1)S(1)}, u32[]{:S(2)}, u32[]{:S(2)}) collective-permute-start(bf16[96,2176]{1,0:T(8,128)(2,1)S(1)} %add_convert_fusion.3), channel_id=1, source_target_pairs={{0,224},{1,33},{2,226},{3,35},{4,228},{5,37},{6,230},{7,39},{8,232... | collective-permute-start | bytes 1253384 | tf_op jit(solution)/shard_map/ppermute | solution.py:294
  156.1 12.7 %collective-permute-start.17 = (bf16[96,2176]{1,0:T(8,128)(2,1)S(1)}, bf16[96,2176]{1,0:T(8,128)(2,1)S(1)}, u32[]{:S(2)}, u32[]{:S(2)}) collective-permute-start(bf16[96,2176]{1,0:T(8,128)(2,1)S(1)} %add_convert_fusion.1), channel_id=1, source_target_pairs={{0,32},{1,225},{2,34},{3,227},{4,36},{5,229},{6,38},{7,231},{8,40}... | collective-permute-start | bytes 1253384 | tf_op jit(solution)/shard_map/ppermute | solution.py:294
  163.7 13.3 %collective-permute-start.14 = (bf16[96,2176]{1,0:T(8,128)(2,1)S(1)}, bf16[96,2176]{1,0:T(8,128)(2,1)S(1)}, u32[]{:S(2)}, u32[]{:S(2)}) collective-permute-start(bf16[96,2176]{1,0:T(8,128)(2,1)S(1)} %add_convert_fusion.2), channel_id=1, source_target_pairs={{0,224},{1,33},{2,226},{3,35},{4,228},{5,37},{6,230},{7,39},{8,232... | collective-permute-start | bytes 1253384 | tf_op jit(solution)/shard_map/ppermute | solution.py:294
  168.9 11.1 %collective-permute-start.18 = (bf16[96,2176]{1,0:T(8,128)(2,1)S(1)}, bf16[96,2176]{1,0:T(8,128)(2,1)S(1)}, u32[]{:S(2)}, u32[]{:S(2)}) collective-permute-start(bf16[96,2176]{1,0:T(8,128)(2,1)S(1)} %add_convert_fusion), channel_id=1, source_target_pairs={{0,32},{1,225},{2,34},{3,227},{4,36},{5,229},{6,38},{7,231},{8,40}... | collective-permute-start | bytes 1253384 | tf_op jit(solution)/shard_map/ppermute | solution.py:294
  181.2 22.3 %all-to-all-start.1 = ((bf16[32,8,896]{2,1,0:T(8,128)(2,1)}), bf16[32,8,896]{2,1,0:T(8,128)(2,1)S(1)}, u32[]{:S(2)}, u32[]{:S(2)}) async-start(bf16[32,8,896]{2,1,0:T(8,128)(2,1)} %bitcast.12), calls=%async_computation.1 | async-start | bytes 917504 | tf_op jit(solution)/shard_map/all_to_all | solution.py:416
  (10 other events, 78.6 us)
